TPU v7x, 256 devices: a whole 4x4x8 slice. The times are simulated.
256 devices in a mesh: tile: 64 (over z, x, core), tm: 4 (over y).
Axes of the slice: x: 4, y: 4, z: 8, core: 2. Of those that a mesh axis runs over, the one named last changes fastest.
Arguments:
- raw: bfloat16 [64, 512, 4, 1039], P('tm', 'tile'), may hold values from -600 to 600
- blocks: int32 [256], P('tile'), may hold values from 0 to 63, as said below
- mask: int32 [8, 256, 8], P('tm', 'tile'), may hold values 0 or 1
Outputs:
- correlations: float32 [8, 256, 8, 512], P('tm', 'tile')
Inputs may be any that keep to these rules, and one draw needn't show every extreme that they name: `blocks`: block r belongs to tile r // 4; its partner is another tile at most 2 tiles away.
All inputs are finite; a program needn't handle non-finite values. No bound on the sum of `mask` on one device may be relied on, other than what follows from the above.
Results may differ from a plain program's by a relative error of at most 0.0077.
Values may be sent and summed in bfloat16 or wider, within the bound.
No kernel may reach another device: no remote copies, remote signals or barrier semaphores. Data moves between devices by JAX's collectives and lax.ppermute only.
A program may use at most 64 MiB of HBM per device.

v0:
```python
import math

import jax
import jax.numpy as jnp
from jax import lax
from jax.sharding import PartitionSpec as P

LAGS = 512
TAPS = 64
DEC = 4
REACH = 2


def shifted(block, axis, distance):
    devices = range(lax.axis_size(axis))
    route = [(i - distance, i) for i in devices if i - distance in devices]
    return lax.ppermute(block, axis, route)


def fir_taps():
    tap_index = jnp.arange(TAPS).astype(jnp.float32)
    centred = (tap_index - (TAPS - 1) / 2.0) / DEC
    taper = 0.5 - 0.5 * jnp.cos(2.0 * jnp.pi * (tap_index + 0.5) / TAPS)
    return (jnp.sinc(centred) * taper / DEC).astype(jnp.float32)


def decimate(samples, filter_taps):
    length = samples.shape[-1] - TAPS // DEC + 1
    total = jnp.zeros(samples.shape[:-2] + (length,), jnp.float32)
    for offset_index in range(TAPS // DEC):
        for phase in range(DEC):
            portion = samples[..., phase, offset_index : offset_index + length].astype(jnp.float32)
            total = total + filter_taps[DEC * offset_index + phase] * portion
    return total.astype(jnp.bfloat16)


def dft_table(length, bins):
    sample_index = jnp.arange(length)[:, None]
    bin_index = jnp.arange(bins)[None, :]
    angle = jnp.mod(sample_index * bin_index, length).astype(jnp.float32) * (2.0 * jnp.pi / length)
    return jnp.concatenate([jnp.cos(angle), -jnp.sin(angle)], axis=1).astype(jnp.bfloat16)


def lag_table(bins, lag_count, length):
    bin_index = jnp.arange(bins)[:, None]
    lag_index = jnp.arange(lag_count)[None, :] - lag_count // 2
    angle = jnp.mod(bin_index * lag_index, length).astype(jnp.float32) * (2.0 * jnp.pi / length)
    weights = jnp.where(bin_index == 0, 1.0, 2.0).astype(jnp.float32)
    return jnp.concatenate([weights * jnp.cos(angle), -weights * jnp.sin(angle)], axis=0)


def band_partial(arranged):
    real_part = arranged[:, :, 0].astype(jnp.float32)
    imag_part = arranged[:, :, 1].astype(jnp.float32)
    return jnp.sum(real_part * real_part + imag_part * imag_part, axis=0)


def fetch_partners(whitened, blocks):
    offsets = [offset for offset in range(-REACH, REACH + 1) if offset != 0]
    received = {}
    for offset in offsets:
        received[offset] = shifted(whitened, "tile", -offset)
    candidates = jnp.stack([received[offset] for offset in offsets], axis=1)
    relative = blocks - lax.axis_index("tile")
    position = jnp.where(relative < 0, relative + REACH, relative + REACH - 1)
    return jnp.take(candidates, position, axis=1)


def cross_spectra(own_spec, partner):
    own_real = own_spec[:, :, None, None, 0].astype(jnp.float32)
    own_imag = own_spec[:, :, None, None, 1].astype(jnp.float32)
    far_real = partner[:, None, :, :, 0].astype(jnp.float32)
    far_imag = partner[:, None, :, :, 1].astype(jnp.float32)
    real_cross = jnp.sum(own_real * far_real + own_imag * far_imag, axis=0)
    imag_cross = jnp.sum(own_imag * far_real - own_real * far_imag, axis=0)
    return jnp.stack([real_cross, imag_cross], axis=3)


def lag_local(stacked, lagtab):
    flattened = stacked.reshape(-1, lagtab.shape[0])
    product = jnp.dot(
        flattened, lagtab, precision=lax.Precision.HIGHEST, preferred_element_type=jnp.float32
    )
    return product.reshape(stacked.shape[0], stacked.shape[1], stacked.shape[2], lagtab.shape[1])


def per_device(raw, blocks, mask):
    windows = raw.shape[0]
    sensors = raw.shape[1]
    length = raw.shape[3] - TAPS // DEC + 1
    bins = length // 2
    groups = lax.axis_size("tm")
    decimated = decimate(raw, fir_taps())
    product = jnp.dot(
        decimated.reshape(windows * sensors, length),
        dft_table(length, bins),
        preferred_element_type=jnp.float32,
    )
    spectra = product.astype(jnp.bfloat16).reshape(windows, sensors, 2, bins)
    lagtab = lag_table(bins, LAGS, length)
    band_sum = lax.psum(band_partial(spectra), "tm")
    amplitude = jnp.sqrt(band_sum / (windows * groups) + 1e-06)
    whitened = (spectra.astype(jnp.float32) / amplitude[None, :, None, :]).astype(jnp.bfloat16)
    partner = fetch_partners(whitened, blocks)
    cross = cross_spectra(whitened, partner)
    stacked = lax.psum_scatter(cross, "tm", scatter_dimension=0, tiled=True)
    lagged = lag_local(stacked, lagtab)
    normaliser = 1.0 / math.sqrt(windows * groups * bins)
    return lagged * normaliser * mask.astype(jnp.float32)[:, :, :, None]


def solution(mesh):
    placed = (P("tm", "tile", None, None), P("tile"), P("tm", "tile", None))
    return jax.shard_map(
        per_device,
        mesh=mesh,
        in_specs=placed,
        out_specs=P("tm", "tile", None, None),
        check_vma=False,
    )
```

profile of v0, /device:TPU:198, one launch (start us, length us, event | category | flops | bytes accessed | tf_op | source)
XLA Modules:
  0.0 235.6 jit_solution(13346105801029474795)
XLA Ops:
  6.6 0.7 fusion.43
  7.3 0.7 fusion.44
  8.0 0.7 fusion.45
  8.8 30.2 %fusion.41 = (bf16[16,8,1,1024]{3,2,1,0:T(2,128)(2,1)S(1)}, bf16[16,8,1,1024]{3,2,1,0:T(2,128)(2,1)S(1)}, bf16[16,8,1,1024]{3,2,1,0:T(2,128)(2,1)S(1)}, bf16[16,...) fusion(bf16[16,8,4,1039]{3,2,1,0:T(4,128)(2,1)} %param.3), kind=kLoop, calls=%fused_computation.128 | loop fusion | bytes 9961472 | tf_op jit(solution)/shard_map/slice | solution.py:32
  39.0 12.3 %fusion.40 = (bf16[16,8,1,1024]{3,2,1,0:T(2,128)(2,1)S(1)}, bf16[16,8,1,1024]{3,2,1,0:T(2,128)(2,1)S(1)}, bf16[16,8,1,1024]{3,2,1,0:T(2,128)(2,1)S(1)}, bf16[16,...) fusion(bf16[16,8,4,1039]{3,2,1,0:T(4,128)(2,1)S(1)} %copy-done), kind=kLoop, calls=%fused_computation.127 | loop fusion | bytes 9961472 | tf_op jit(solution)/shard_map/slice | solution.py:32
  51.3 12.4 %fusion.39 = (bf16[16,8,1,1024]{3,2,1,0:T(2,128)(2,1)S(1)}, bf16[16,8,1,1024]{3,2,1,0:T(2,128)(2,1)S(1)}, bf16[16,8,1,1024]{3,2,1,0:T(2,128)(2,1)S(1)}, bf16[16,...) fusion(bf16[16,8,4,1039]{3,2,1,0:T(4,128)(2,1)S(1)} %copy-done), kind=kLoop, calls=%fused_computation.126 | loop fusion | bytes 9961472 | tf_op jit(solution)/shard_map/slice | solution.py:32
  63.7 0.7 fusion.46
  64.4 6.3 %fusion.42 = (bf16[16,8,1,1024]{3,2,1,0:T(2,128)(2,1)S(1)}, bf16[16,8,1,1024]{3,2,1,0:T(2,128)(2,1)S(1)}, bf16[16,8,1,1024]{3,2,1,0:T(2,128)(2,1)S(1)}, bf16[16,...) fusion(bf16[16,8,4,1039]{3,2,1,0:T(4,128)(2,1)S(1)} %copy-done), kind=kLoop, calls=%fused_computation.129 | loop fusion | bytes 3670016 | tf_op jit(solution)/shard_map/slice | solution.py:32
  70.7 8.5 %negate_convert_fusion = (bf16[1024,512]{1,0:T(8,128)(2,1)S(1)}, bf16[1024,512]{1,0:T(8,128)(2,1)S(1)}) fusion(), kind=kLoop, calls=%fused_computation.17 | loop fusion | flops 8912896 | bytes 2097152 | tf_op jit(solution)/shard_map/convert.5
  83.2 46.0 %fusion.13 = bf16[128,1024]{1,0:T(8,128)(2,1)S(1)} fusion(bf16[1024,512]{1,0:T(8,128)(2,1)S(1)} %get-tuple-element.143, bf16[1024,512]{1,0:T(8,128)(2,1)S(1)} %get-tuple-element.144, bf16[16,8,1,1024]{3,1,0,2:T(8,128)(2,1)S(1)} %copy.317, bf16[16,8,1,1024]{3,1,0,2:T(8,128)(2,1)S(1)} %copy.316, bf16[16,8,1,1024]{3,1,0,2:T(8,128)(2,1)S(1)} %copy.315, ...), kind=kOutput, calls=%fused_computation.25 | convolution fusion | flops 297926656 | bytes 19136768 | tf_op jit(solution)/shard_map/dot_general | solution.py:94
  129.2 17.2 %psum.7 = f32[8,512]{1,0:T(8,128)S(1)} all-reduce(f32[8,512]{1,0:T(8,128)S(1)} %add_reduce_fusion.1), channel_id=1, replica_groups=mesh['tile'=64,'tm'=4] {'tm'}, use_global_device_ids=true, to_apply=%region_1.2 | all-reduce | flops 4096 | bytes 32768 | tf_op jit(solution)/shard_map/psum | solution.py:101
  146.4 2.8 %collective-permute-start = (bf16[16,8,2,512]{3,1,2,0:T(8,128)(2,1)S(1)}, bf16[16,8,2,512]{3,1,2,0:T(8,128)(2,1)S(1)}, u32[]{:S(2)}, u32[]{:S(2)}) collective-permute-start(bf16[16,8,2,512]{3,1,2,0:T(8,128)(2,1)S(1)} %divide_convert_fusion), channel_id=1, source_target_pairs={{0,8},{4,12},{8,16},{12,20},{16,24},{20,28},{24,32},{28,36},{32,40... | collective-permute-start | bytes 786440 | tf_op jit(solution)/shard_map/ppermute | solution.py:17
  149.3 1.9 collective-permute-start.1
  151.2 3.6 %collective-permute-start.2 = (bf16[16,8,2,512]{3,1,2,0:T(8,128)(2,1)S(1)}, bf16[16,8,2,512]{3,1,2,0:T(8,128)(2,1)S(1)}, u32[]{:S(2)}, u32[]{:S(2)}) collective-permute-start(bf16[16,8,2,512]{3,1,2,0:T(8,128)(2,1)S(1)} %divide_convert_fusion), channel_id=1, source_target_pairs={{4,0},{8,4},{12,8},{16,12},{20,16},{24,20},{28,24},{32,28},{36,32}... | collective-permute-start | bytes 786440 | tf_op jit(solution)/shard_map/ppermute | solution.py:17
  154.9 3.0 %collective-permute-start.3 = (bf16[16,8,2,512]{3,1,2,0:T(8,128)(2,1)S(1)}, bf16[16,8,2,512]{3,1,2,0:T(8,128)(2,1)S(1)}, u32[]{:S(2)}, u32[]{:S(2)}) collective-permute-start(bf16[16,8,2,512]{3,1,2,0:T(8,128)(2,1)S(1)} %divide_convert_fusion), channel_id=1, source_target_pairs={{8,0},{12,4},{16,8},{20,12},{24,16},{28,20},{32,24},{36,28},{40,32... | collective-permute-start | bytes 786440 | tf_op jit(solution)/shard_map/ppermute | solution.py:17
  158.0 2.1 collective-permute-done.2
  160.1 8.3 %collective-permute-done.3 = bf16[16,8,2,512]{3,1,2,0:T(8,128)(2,1)S(1)} collective-permute-done((bf16[16,8,2,512]{3,1,2,0:T(8,128)(2,1)S(1)}, bf16[16,8,2,512]{3,1,2,0:T(8,128)(2,1)S(1)}, u32[]{:S(2)}, u32[]{:S(2)}) %collective-permute-start.3) | collective-permute-done | bytes 262176 | tf_op jit(solution)/shard_map/ppermute | solution.py:17
  168.5 0.6 gather_fusion
  169.6 5.0 %add_reduce_fusion = (f32[8,4,8,512]{3,2,1,0:T(8,128)S(1)}, f32[8,4,8,512]{3,2,1,0:T(8,128)S(1)}) fusion(f32[16,8,512]{2,1,0:T(8,128)S(1)} %get-tuple-element.76, f32[16,8,512]{2,1,0:T(8,128)S(1)} %get-tuple-element.75, f32[16,4,8,512]{3,2,0,1:T(8,128)S(1)} %get-tuple-element.73, f32[16,4,8,512]{3,2,0,1:T(8,128)S(1)} %get-tuple-element.74), kind=kLoop, calls=%fused_computation.2 | loop fusion | flops 16515072 | bytes 3670016 | tf_op jit(solution)/shard_map/reduce_sum | solution.py:74
  174.6 1.1 pad_maximum_fusion.1
  177.0 4.2 %cosine_multiply_fusion = (f32[512,512]{1,0:T(8,128)S(1)}, f32[512,512]{1,0:T(8,128)S(1)}) fusion(s32[512]{0:T(512)S(1)} %iota_add_fusion, f32[512]{0:T(512)S(1)} %get-tuple-element.145, f32[512]{0:T(512)S(1)} %get-tuple-element.146), kind=kLoop, calls=%fused_computation.34 | loop fusion | flops 4194304 | bytes 2103296 | tf_op jit(solution)/shard_map/mul | solution.py:49
  181.2 44.5 %all-reduce.3.cloned.1.call-done = f32[8,4,8,2,512]{4,2,1,0,3:T(8,128)} async-done(((f32[8,4,8,2,512]{4,2,1,0,3:T(8,128)}), f32[8,4,8,2,512]{4,2,1,0,3:T(8,128)}) %all-reduce.3.cloned.1.call-update) | async-done | bytes 1048592
  225.7 1.0 dynamic-slice_bitcast_fusion
  226.7 2.0 fusion.16
  (70 shorter events, 5.1 us)
Async XLA Ops:
  6.5 219.2 %all-reduce.3.cloned.1.call-start = ((), (), s32[]{:S(2)}) async-start(), calls=%async_computation | async-start | bytes 2097152
  8.8 30.2 %copy-start = (bf16[16,8,4,1039]{3,2,1,0:T(4,128)(2,1)S(1)}, bf16[16,8,4,1039]{3,2,1,0:T(4,128)(2,1)}, u32[]{:S(2)}) copy-start(bf16[16,8,4,1039]{3,2,1,0:T(4,128)(2,1)} %param.3) | copy-start | bytes 3191812
  83.1 74.7 %copy-start.2 = (s32[4]{0:T(128)S(1)}, s32[4]{0:T(128)}, u32[]{:S(2)}) copy-start(s32[4]{0:T(128)} %param.4) | copy-start | bytes 52
  146.4 11.5 %collective-permute-start = (bf16[16,8,2,512]{3,1,2,0:T(8,128)(2,1)S(1)}, bf16[16,8,2,512]{3,1,2,0:T(8,128)(2,1)S(1)}, u32[]{:S(2)}, u32[]{:S(2)}) collective-permute-start(bf16[16,8,2,512]{3,1,2,0:T(8,128)(2,1)S(1)} %divide_convert_fusion), channel_id=1, source_target_pairs={{0,8},{4,12},{8,16},{12,20},{16,24},{20,28},{24,32},{28,36},{32,40... | collective-permute-start | bytes 786440 | tf_op jit(solution)/shard_map/ppermute | solution.py:17
  149.3 8.7 %collective-permute-start.1 = (bf16[16,8,2,512]{3,1,2,0:T(8,128)(2,1)S(1)}, bf16[16,8,2,512]{3,1,2,0:T(8,128)(2,1)S(1)}, u32[]{:S(2)}, u32[]{:S(2)}) collective-permute-start(bf16[16,8,2,512]{3,1,2,0:T(8,128)(2,1)S(1)} %divide_convert_fusion), channel_id=1, source_target_pairs={{0,4},{4,8},{8,12},{12,16},{16,20},{20,24},{24,28},{28,32},{32,36}... | collective-permute-start | bytes 786440 | tf_op jit(solution)/shard_map/ppermute | solution.py:17
  151.2 8.9 %collective-permute-start.2 = (bf16[16,8,2,512]{3,1,2,0:T(8,128)(2,1)S(1)}, bf16[16,8,2,512]{3,1,2,0:T(8,128)(2,1)S(1)}, u32[]{:S(2)}, u32[]{:S(2)}) collective-permute-start(bf16[16,8,2,512]{3,1,2,0:T(8,128)(2,1)S(1)} %divide_convert_fusion), channel_id=1, source_target_pairs={{4,0},{8,4},{12,8},{16,12},{20,16},{24,20},{28,24},{32,28},{36,32}... | collective-permute-start | bytes 786440 | tf_op jit(solution)/shard_map/ppermute | solution.py:17
  154.9 13.5 %collective-permute-start.3 = (bf16[16,8,2,512]{3,1,2,0:T(8,128)(2,1)S(1)}, bf16[16,8,2,512]{3,1,2,0:T(8,128)(2,1)S(1)}, u32[]{:S(2)}, u32[]{:S(2)}) collective-permute-start(bf16[16,8,2,512]{3,1,2,0:T(8,128)(2,1)S(1)} %divide_convert_fusion), channel_id=1, source_target_pairs={{8,0},{12,4},{16,8},{20,12},{24,16},{28,20},{32,24},{36,28},{40,32... | collective-permute-start | bytes 786440 | tf_op jit(solution)/shard_map/ppermute | solution.py:17
  174.6 1.1 copy-start.3
  174.6 2.4 %copy-start.1 = (s32[2,4,8]{2,1,0:T(4,128)S(1)}, s32[2,4,8]{2,1,0:T(4,128)}, u32[]{:S(2)}) copy-start(s32[2,4,8]{2,1,0:T(4,128)} %param.5) | copy-start | bytes 772
Sparse Core Ops, SparseCore 0:
  175.9 49.7 all-reduce.2
where the time goes:
time: 239 us; the launch traced here: 236 us
  local copies, waits for them, and re-layouts  69.9 us (29%)
  waiting for transfers between devices  54.9 us (23%)
  matrix products  48 us (20%)
  other arithmetic  19.6 us (8%)
  blocking collectives  17.2 us (7%)
  between operations  14.6 us (6%)
  starting transfers between devices  11.4 us (5%)
    slice x4, local copies, waits for them, and re-layouts, decimate(): samples[..., phase, offset_index:offset_index + length].astype(jnp.float32)  61.2 us
    dot_general x1, matrix products, per_device(): jnp.dot(decimated.reshape(windows * sensors, length), dft_table(length, b...  46 us
    unnamed x2, waiting for transfers between devices  44.5 us
    psum x1, blocking collectives, per_device(): band_sum = lax.psum(band_partial(spectra), 'tm')  17.2 us
    ppermute x4, starting transfers between devices, shifted(): return lax.ppermute(block, axis, route)  11.4 us
    ppermute x4, waiting for transfers between devices, shifted(): return lax.ppermute(block, axis, route)  10.4 us
    another operation x1, other arithmetic  8.54 us
    unnamed x53, local copies, waits for them, and re-layouts  5.22 us
  transfers between devices with their start and end apart: 5, of which 3 were waited for; matrix products, arithmetic and copies ran while one was open for 2% of the time, Pallas kernels for 0%

commit v1 on v0

v1 whole, which is shorter than its diff:
```python
import functools
import math

import jax
import jax.numpy as jnp
import ml_dtypes
import numpy as np
from jax import lax
from jax.experimental import pallas as pl
from jax.experimental.pallas import tpu as pltpu
from jax.sharding import PartitionSpec as P

LAGS = 512
TAPS = 64
DEC = 4
REACH = 2
BINS = 512
LENGTH = 2 * BINS
SENSORS = 8
WIN = 16
ROWS = WIN * SENSORS
LANE = 128
SCALE = 2.0**32
PAIRS = 2 * SENSORS
CANDS = 4
MESSAGE = CANDS * PAIRS + 32
VMEM = pltpu.MemorySpace.VMEM
LIMIT = 48 * 1024 * 1024
bf16 = jnp.bfloat16
f32 = jnp.float32


def split_high_low(values):
    high = values.astype(ml_dtypes.bfloat16)
    low = (values - high.astype(np.float32)).astype(ml_dtypes.bfloat16)
    return high, low


def fir_table():
    index = np.arange(TAPS).astype(np.float64)
    centred = (index - (TAPS - 1) / 2.0) / DEC
    taper = 0.5 - 0.5 * np.cos(2.0 * np.pi * (index + 0.5) / TAPS)
    taps = (np.sinc(centred) * taper / DEC).astype(np.float32)
    high, low = split_high_low(taps)
    table = np.zeros((DEC, 2 * LANE, 2 * LANE), ml_dtypes.bfloat16)
    column = np.arange(LANE)
    for phase in range(DEC):
        for offset in range(TAPS // DEC):
            table[phase, column + offset, column] = high[DEC * offset + phase]
            table[phase, column + offset, LANE + column] = low[DEC * offset + phase]
    return table


def dft_table():
    sample = np.arange(LENGTH)[:, None]
    bins = np.arange(BINS)[None, :]
    angle = np.mod(sample * bins, LENGTH).astype(np.float64) * (2.0 * np.pi / LENGTH)
    table = np.concatenate([np.cos(angle), -np.sin(angle)], axis=1).astype(np.float32)
    return (table.astype(ml_dtypes.bfloat16).astype(np.float32) * np.float32(SCALE)).astype(
        ml_dtypes.bfloat16
    )


def lag_table():
    bins = np.arange(BINS)[:, None]
    lag = np.arange(LAGS)[None, :] - LAGS // 2
    angle = np.mod(bins * lag, LENGTH).astype(np.float64) * (2.0 * np.pi / LENGTH)
    weights = np.where(bins == 0, 1.0, 2.0)
    table = np.concatenate([weights * np.cos(angle), -weights * np.sin(angle)], axis=0)
    high, low = split_high_low(table.astype(np.float32))
    return np.stack([high, low])


def spectra_kernel(raw_ref, fir_ref, dft_ref, out_ref, wide_ref):
    blocks = LENGTH // LANE
    tail = raw_ref.shape[-1] - LENGTH
    wide_ref[blocks] = jnp.zeros((DEC * ROWS, LANE), f32)
    for row in range(ROWS):
        place = slice(row * DEC, (row + 1) * DEC)
        values = raw_ref[row // SENSORS, row % SENSORS].astype(f32)
        for k in range(blocks):
            wide_ref[k, place] = values[:, LANE * k : LANE * (k + 1)]
        wide_ref[blocks, place, :tail] = values[:, LENGTH:]
    total = jnp.zeros((SENSORS * ROWS, 2 * LANE), f32)
    for phase in range(DEC):
        samples = [
            wide_ref[k, pl.ds(phase, ROWS, stride=DEC), :].astype(bf16) for k in range(blocks + 1)
        ]
        stacked = jnp.concatenate(
            [jnp.concatenate(samples[k : k + 2], axis=1) for k in range(blocks)], axis=0
        )
        total = total + jnp.dot(stacked, fir_ref[phase], preferred_element_type=f32)
    summed = (total[:, :LANE] + total[:, LANE:]).astype(bf16)
    decimated = jnp.concatenate(
        [summed[ROWS * k : ROWS * (k + 1)] for k in range(blocks)], axis=1
    )
    out_ref[...] = jnp.dot(decimated, dft_ref[...], preferred_element_type=f32).astype(bf16)


def spectra_of(raw):
    return pl.pallas_call(
        spectra_kernel,
        out_shape=jax.ShapeDtypeStruct((ROWS, LENGTH), bf16),
        in_specs=[pl.BlockSpec(memory_space=VMEM)] * 3,
        out_specs=pl.BlockSpec(memory_space=VMEM),
        scratch_shapes=[pltpu.VMEM((LENGTH // LANE + 1, DEC * ROWS, LANE), f32)],
        compiler_params=pltpu.CompilerParams(vmem_limit_bytes=LIMIT),
        cost_estimate=pl.CostEstimate(flops=2 * 10**9, bytes_accessed=5 * 10**6, transcendentals=0),
        name="spectra",
    )(raw, jnp.asarray(fir_table()), jnp.asarray(dft_table()))


def cross_body(own_ref, far_ref, store):
    for tile in range(BINS // LANE):
        real = slice(LANE * tile, LANE * (tile + 1))
        imag = slice(BINS + LANE * tile, BINS + LANE * (tile + 1))

        def step(pair, totals):
            first, second, third, power = totals
            rows = pl.ds(pl.multiple_of(pair * 16, 16), 16)
            own_real = own_ref[rows, real].astype(f32)
            own_imag = own_ref[rows, imag].astype(f32)
            far_real = far_ref[rows, real].astype(f32)
            far_imag = far_ref[rows, imag].astype(f32)
            own_sum = own_real + own_imag
            far_difference = far_real - far_imag
            first, second, third = list(first), list(second), list(third)
            for half in range(2):
                part = slice(SENSORS * half, SENSORS * (half + 1))
                power = power + (far_real[part] * far_real[part] + far_imag[part] * far_imag[part])
                for i in range(SENSORS):
                    row = SENSORS * half + i
                    first[i] = first[i] + own_real[row : row + 1] * far_real[part]
                    second[i] = second[i] + own_imag[row : row + 1] * far_imag[part]
                    third[i] = third[i] + own_sum[row : row + 1] * far_difference[part]
            return tuple(first), tuple(second), tuple(third), power

        zero = jnp.zeros((SENSORS, LANE), f32)
        zeros = (zero,) * SENSORS
        first, second, third, power = lax.fori_loop(
            0, WIN // 2, step, (zeros, zeros, zeros, zero), unroll=True
        )
        store(real, imag, first, second, third, power)


def put_cross(out_ref, base, real, imag, first, second, third):
    for y in range(4):
        pair = [2 * y, 2 * y + 1]
        real_cross = jnp.concatenate([first[i] + second[i] for i in pair], axis=0)
        imag_cross = jnp.concatenate([third[i] - first[i] + second[i] for i in pair], axis=0)
        out_ref[y, base : base + PAIRS, real] = real_cross.astype(bf16)
        out_ref[y, base : base + PAIRS, imag] = imag_cross.astype(bf16)


def cross_kernel(own_ref, far_ref, out_ref, power_ref):
    def store(real, imag, first, second, third, power):
        put_cross(out_ref, 0, real, imag, first, second, third)
        power_ref[:, real] = power

    cross_body(own_ref, far_ref, store)


def cross_of(own, far):
    return pl.pallas_call(
        cross_kernel,
        out_shape=(
            jax.ShapeDtypeStruct((4, PAIRS, LENGTH), bf16),
            jax.ShapeDtypeStruct((SENSORS, BINS), f32),
        ),
        in_specs=[pl.BlockSpec(memory_space=VMEM)] * 2,
        out_specs=(pl.BlockSpec(memory_space=VMEM),) * 2,
        compiler_params=pltpu.CompilerParams(vmem_limit_bytes=LIMIT),
        cost_estimate=pl.CostEstimate(flops=10**8, bytes_accessed=10**6, transcendentals=0),
        name="cross",
    )(own, far)


def message_kernel(own_ref, third_ref, fourth_ref, s_ref, sp_ref, a_ref, ap_ref, out_ref):
    for y in range(4):
        out_ref[y, 0:PAIRS] = s_ref[y]
        out_ref[y, PAIRS : 2 * PAIRS] = a_ref[y]
    base = CANDS * PAIRS
    own_power = jnp.zeros((SENSORS, BINS), f32)
    for w in range(WIN // 2):
        block = own_ref[16 * w : 16 * (w + 1)].astype(f32)
        square = block * block
        square = square[:SENSORS] + square[SENSORS:]
        own_power = own_power + (square[:, :BINS] + square[:, BINS:])
    powers = {0: sp_ref[...], 1: ap_ref[...]}
    for slot, far_ref in ((2, third_ref), (3, fourth_ref)):
        collected = []

        def store(real, imag, first, second, third, power):
            put_cross(out_ref, slot * PAIRS, real, imag, first, second, third)
            collected.append(power)

        cross_body(own_ref, far_ref, store)
        powers[slot] = jnp.concatenate(collected, axis=1)
    near = jnp.concatenate(
        [
            jnp.concatenate([powers[0], powers[1]], axis=1),
            jnp.concatenate([powers[2], powers[3]], axis=1),
        ],
        axis=0,
    ).astype(bf16)
    high = own_power.astype(bf16)
    low = (own_power - high.astype(f32)).astype(bf16)
    mine = jnp.concatenate([high, low], axis=1)
    mine = jnp.concatenate([mine, mine], axis=0)
    for y in range(4):
        out_ref[y, base : base + 16] = near
        out_ref[y, base + 16 : base + 32] = mine


def message_of(own, third, fourth, s_cross, s_power, a_cross, a_power):
    return pl.pallas_call(
        message_kernel,
        out_shape=jax.ShapeDtypeStruct((4, MESSAGE, LENGTH), bf16),
        in_specs=[pl.BlockSpec(memory_space=VMEM)] * 7,
        out_specs=pl.BlockSpec(memory_space=VMEM),
        compiler_params=pltpu.CompilerParams(vmem_limit_bytes=LIMIT),
        cost_estimate=pl.CostEstimate(flops=2 * 10**8, bytes_accessed=10**6, transcendentals=0),
        name="message",
    )(own, third, fourth, s_cross, s_power, a_cross, a_power)


def lag_kernel(slots_ref, position_ref, got_ref, table_ref, mask_ref, out_ref, lagged_ref):
    base = CANDS * PAIRS

    def summed(rows):
        return (got_ref[0, rows].astype(f32) + got_ref[1, rows].astype(f32)) + (
            got_ref[2, rows].astype(f32) + got_ref[3, rows].astype(f32)
        )

    def inverse(power):
        return lax.rsqrt(power / (4 * WIN) + 1e-06 * SCALE * SCALE)

    near = inverse(summed(slice(base, base + 16)))
    mine = summed(slice(base + 16, base + 32))[:SENSORS]
    mine = inverse(mine[:, :BINS] + mine[:, BINS:])
    y = position_ref[0]
    sensor = lax.broadcasted_iota(jnp.int32, (SENSORS, BINS), 0)
    own = [
        jnp.sum(jnp.where(sensor == 2 * y + i, mine, 0.0), axis=0, keepdims=True) for i in range(2)
    ]
    pieces = []
    for slot in range(CANDS):
        row, column = slot // 2, slot % 2
        far = near[SENSORS * row : SENSORS * (row + 1), BINS * column : BINS * (column + 1)]
        cross = summed(slice(slot * PAIRS, (slot + 1) * PAIRS))
        for i in range(2):
            factor = far * own[i]
            factor = jnp.concatenate([factor, factor], axis=1)
            pieces.append(cross[SENSORS * i : SENSORS * (i + 1)] * factor)
    whitened = jnp.concatenate(pieces, axis=0)
    high = whitened.astype(bf16)
    low = (whitened - high.astype(f32)).astype(bf16)
    lagged = jnp.dot(high, table_ref[0], preferred_element_type=f32)
    lagged = lagged + jnp.dot(high, table_ref[1], preferred_element_type=f32)
    lagged = lagged + jnp.dot(low, table_ref[0], preferred_element_type=f32)
    lagged_ref[...] = lagged.reshape(CANDS, 2, SENSORS, LAGS)
    normaliser = 1.0 / math.sqrt(4 * WIN * BINS)
    for r in range(4):
        slot = slots_ref[r]
        for i in range(2):
            factor = mask_ref[i, r] * normaliser
            for k in range(LAGS // LANE):
                lanes = slice(LANE * k, LANE * (k + 1))
                out_ref[i, r, :, lanes] = lagged_ref[slot, i, :, lanes] * factor


def lag_of(slots, position, got, mask):
    smem = pl.BlockSpec(memory_space=pltpu.MemorySpace.SMEM)
    vmem = pl.BlockSpec(memory_space=VMEM)
    return pl.pallas_call(
        lag_kernel,
        out_shape=jax.ShapeDtypeStruct((2, 4, SENSORS, LAGS), f32),
        in_specs=[smem, smem, vmem, vmem, vmem],
        out_specs=vmem,
        scratch_shapes=[pltpu.VMEM((CANDS, 2, SENSORS, LAGS), f32)],
        compiler_params=pltpu.CompilerParams(vmem_limit_bytes=LIMIT),
        cost_estimate=pl.CostEstimate(flops=2 * 10**8, bytes_accessed=3 * 10**6, transcendentals=0),
        name="lag",
    )(slots, position, got, jnp.asarray(lag_table()), mask)


def per_device(raw, blocks, mask):
    tiles = lax.axis_size("tile")
    tile = lax.axis_index("tile")
    core = tile % 2
    relative = blocks - tile
    other = 1 - 2 * core
    slots = jnp.where(
        relative == other,
        0,
        jnp.where(relative == -other, 3, jnp.where(relative == 2 * other, 1, 2)),
    ).astype(jnp.int32)
    position = lax.axis_index("tm").astype(jnp.int32).reshape(1)
    wide_mask = jnp.broadcast_to(mask.astype(f32)[..., None], mask.shape + (LANE,))

    def ring(block, distances):
        route = [(i, (i + distances[i % 2]) % tiles) for i in range(tiles)]
        return lax.ppermute(block, "tile", route)

    spectra = spectra_of(raw)
    near = ring(spectra, (1, -1))
    ahead = ring(spectra, (-2, 2))
    behind = ring(spectra, (2, -2))
    corner = ring(ahead, (1, -1))
    s_cross, s_power = cross_of(spectra, near)
    a_cross, a_power = cross_of(spectra, ahead)
    message = message_of(spectra, behind, corner, s_cross, s_power, a_cross, a_power)
    got = lax.all_to_all(message, "tm", 0, 0)
    return lag_of(slots, position, got, wide_mask)


def solution(mesh):
    placed = (P("tm", "tile", None, None), P("tile"), P("tm", "tile", None))
    return jax.shard_map(
        per_device,
        mesh=mesh,
        in_specs=placed,
        out_specs=P("tm", "tile", None, None),
        check_vma=False,
    )
```

time: 239 us -> 42.7 us (0.18)
  the two profiles are of different devices: /device:TPU:198 before, /device:TPU:8 now
where the time goes in v1:
time: 42.7 us; the launch traced here: 42.4 us
  waiting for transfers between devices  17.9 us (42%)
  starting transfers between devices  13 us (30%)
  Pallas kernels  7.41 us (17%)
  local copies, waits for them, and re-layouts  3.99 us (9%)
    all_to_all x1, waiting for transfers between devices, per_device(): got = lax.all_to_all(message, 'tm', 0, 0)  9.7 us
    ppermute x4, waiting for transfers between devices, ring(): return lax.ppermute(block, 'tile', route)  8.21 us
    ppermute x4, starting transfers between devices, ring(): return lax.ppermute(block, 'tile', route)  8.14 us
    all_to_all x1, starting transfers between devices, per_device(): got = lax.all_to_all(message, 'tm', 0, 0)  4.91 us
    unnamed x12, local copies, waits for them, and re-layouts  3.92 us
    pallas_call x1, Pallas kernels, message_of(): pl.pallas_call(message_kernel, out_shape=jax.ShapeDtypeStruct((4, MESSAGE...  2.39 us
    pallas_call x1, Pallas kernels, lag_of(): pl.pallas_call(lag_kernel, out_shape=jax.ShapeDtypeStruct((2, 4, SENSORS,...  1.89 us
    pallas_call x1, Pallas kernels, spectra_of(): pl.pallas_call(spectra_kernel, out_shape=jax.ShapeDtypeStruct((ROWS, LENG...  1.7 us
  transfers between devices with their start and end apart: 5, of which 3 were waited for; matrix products, arithmetic and copies ran while one was open for 0% of the time, Pallas kernels for 3%

profile of v1, /device:TPU:8, one launch (start us, length us, event | category | flops | bytes accessed | tf_op | source)
XLA Modules:
  0.0 42.4 jit_solution(1086932721825796139)
XLA Ops:
  0.0 1.3 %copy-done.1 = bf16[16,8,4,1039]{3,2,1,0:T(4,128)(2,1)S(1)} copy-done((bf16[16,8,4,1039]{3,2,1,0:T(4,128)(2,1)S(1)}, bf16[16,8,4,1039]{3,2,1,0:T(4,128)(2,1)}, u32[]{:S(2)}) %copy-start.1) | copy-done | bytes 1063960
  1.3 1.6 %copy-done.2 = bf16[1024,1024]{1,0:T(8,128)(2,1)S(1)} copy-done((bf16[1024,1024]{1,0:T(8,128)(2,1)S(1)}, bf16[1024,1024]{1,0:T(8,128)(2,1)}, u32[]{:S(2)}) %copy-start.2) | copy-done | bytes 2097176
  2.9 1.0 %copy-done.3 = bf16[4,256,256]{2,1,0:T(8,128)(2,1)S(1)} copy-done((bf16[4,256,256]{2,1,0:T(8,128)(2,1)S(1)}, bf16[4,256,256]{2,1,0:T(8,128)(2,1)}, u32[]{:S(2)}) %copy-start.3) | copy-done | bytes 524312
  3.9 1.7 %spectra.1.own_ref = bf16[128,1024]{1,0:T(8,128)(2,1)S(1)} custom-call(bf16[16,8,4,1039]{3,2,1,0:T(4,128)(2,1)S(1)} %copy-done.1, bf16[4,256,256]{2,1,0:T(8,128)(2,1)S(1)} %copy-done.3, bf16[1024,1024]{1,0:T(8,128)(2,1)S(1)} %copy-done.2), custom_call_target="tpu_custom_call" | custom-call | flops 2000000000 | bytes 5000000 | tf_op jit(solution)/shard_map/spectra/pallas_call | solution.py:101
  5.6 8.1 %collective-permute-start.1 = (bf16[128,1024]{1,0:T(8,128)(2,1)S(1)}, bf16[128,1024]{1,0:T(8,128)(2,1)S(1)}, u32[]{:S(2)}, u32[]{:S(2)}) collective-permute-start(bf16[128,1024]{1,0:T(8,128)(2,1)S(1)} %spectra.1.own_ref), channel_id=1, source_target_pairs={{0,248},{4,12},{8,0},{12,20},{16,8},{20,28},{24,16},{28,36},{32,24... | collective-permute-start | bytes 786440 | tf_op jit(solution)/shard_map/ppermute | solution.py:303
  13.7 0.0 collective-permute-start.3
  13.7 0.0 collective-permute-start
  13.7 6.4 %collective-permute-done.1.far_ref = bf16[128,1024]{1,0:T(8,128)(2,1)S(1)} collective-permute-done((bf16[128,1024]{1,0:T(8,128)(2,1)S(1)}, bf16[128,1024]{1,0:T(8,128)(2,1)S(1)}, u32[]{:S(2)}, u32[]{:S(2)}) %collective-permute-start.1) | collective-permute-done | bytes 262176 | tf_op jit(solution)/shard_map/ppermute | solution.py:303
  20.2 0.0 collective-permute-start.2
  20.2 0.7 %cross.3 = (bf16[4,16,1024]{2,1,0:T(8,128)(2,1)S(1)}, f32[8,512]{1,0:T(8,128)S(1)}) custom-call(bf16[128,1024]{1,0:T(8,128)(2,1)S(1)} %spectra.1.own_ref, bf16[128,1024]{1,0:T(8,128)(2,1)S(1)} %collective-permute-done.1.far_ref), custom_call_target="tpu_custom_call" | custom-call | flops 100000000 | bytes 1000000 | tf_op jit(solution)/shard_map/cross/pallas_call | solution.py:164
  20.9 0.0 copy-start.4
  20.9 0.0 copy-start.5
  20.9 0.0 copy-start
  20.9 0.0 collective-permute-done.3.far_ref
  20.9 0.7 %cross.2 = (bf16[4,16,1024]{2,1,0:T(8,128)(2,1)S(1)}, f32[8,512]{1,0:T(8,128)S(1)}) custom-call(bf16[128,1024]{1,0:T(8,128)(2,1)S(1)} %spectra.1.own_ref, bf16[128,1024]{1,0:T(8,128)(2,1)S(1)} %collective-permute-done.3.far_ref), custom_call_target="tpu_custom_call" | custom-call | flops 100000000 | bytes 1000000 | tf_op jit(solution)/shard_map/cross/pallas_call | solution.py:164
  21.6 1.8 %collective-permute-done.third_ref = bf16[128,1024]{1,0:T(8,128)(2,1)S(1)} collective-permute-done((bf16[128,1024]{1,0:T(8,128)(2,1)S(1)}, bf16[128,1024]{1,0:T(8,128)(2,1)S(1)}, u32[]{:S(2)}, u32[]{:S(2)}) %collective-permute-start) | collective-permute-done | bytes 262176 | tf_op jit(solution)/shard_map/ppermute | solution.py:303
  23.4 0.0 collective-permute-done.2.fourth_ref
  23.4 2.4 %message.1 = bf16[4,96,1024]{2,1,0:T(8,128)(2,1)} custom-call(bf16[128,1024]{1,0:T(8,128)(2,1)S(1)} %spectra.1.own_ref, bf16[128,1024]{1,0:T(8,128)(2,1)S(1)} %collective-permute-done.third_ref, bf16[128,1024]{1,0:T(8,128)(2,1)S(1)} %collective-permute-done.2.fourth_ref, bf16[4,16,1024]{2,1,0:T(8,128)(2,1)S(1)} %get-tuple-element.9.s_ref, ...), custom_call_target="tpu_custom_call" | custom-call | flops 200000000 | bytes 1000000 | tf_op jit(solution)/shard_map/message/pallas_call | solution.py:216
  25.8 4.9 %all-to-all-start = ((bf16[4,96,1024]{2,1,0:T(8,128)(2,1)}), bf16[4,96,1024]{2,1,0:T(8,128)(2,1)S(1)}, u32[]{:S(2)}, u32[]{:S(2)}) async-start(bf16[4,96,1024]{2,1,0:T(8,128)(2,1)} %message.1), calls=%async_computation | async-start | bytes 1572864 | tf_op jit(solution)/shard_map/all_to_all | solution.py:313
  30.7 0.0 copy-done.4
  30.8 9.7 %all-to-all-done.got_ref = bf16[4,96,1024]{2,1,0:T(8,128)(2,1)S(1)} async-done(((bf16[4,96,1024]{2,1,0:T(8,128)(2,1)}), bf16[4,96,1024]{2,1,0:T(8,128)(2,1)S(1)}, u32[]{:S(2)}, u32[]{:S(2)}) %all-to-all-start) | async-done | bytes 786464 | tf_op jit(solution)/shard_map/all_to_all | solution.py:313
  40.5 0.1 broadcast_in_dim.25.mask_ref
  40.5 0.0 copy-done
  40.5 1.9 %lag.1 = f32[2,4,8,512]{3,2,1,0:T(8,128)} custom-call(s32[4]{0:T(128)S(1)} %compare_select_fusion.2.slots_ref, s32[1]{0:T(128)} %bitcast.position_ref, bf16[4,96,1024]{2,1,0:T(8,128)(2,1)S(1)} %all-to-all-done.got_ref, bf16[2,1024,512]{2,1,0:T(8,128)(2,1)S(1)} %copy-done, f32[2,4,8,128]{3,2,1,0:T(8,128)S(1)} %broadcast_in_dim.25.mask_ref), custom_call_target="tpu_custom_call" | custom-call | flops 200000000 | bytes 3000000 | tf_op jit(solution)/shard_map/lag/pallas_call | solution.py:275
  (6 shorter events, 0.0 us)
Async XLA Ops:
  0.0 1.3 %copy-start.1 = (bf16[16,8,4,1039]{3,2,1,0:T(4,128)(2,1)S(1)}, bf16[16,8,4,1039]{3,2,1,0:T(4,128)(2,1)}, u32[]{:S(2)}) copy-start(bf16[16,8,4,1039]{3,2,1,0:T(4,128)(2,1)} %raw_ref.1) | copy-start | bytes 3191812
  1.3 1.6 %copy-start.2 = (bf16[1024,1024]{1,0:T(8,128)(2,1)S(1)}, bf16[1024,1024]{1,0:T(8,128)(2,1)}, u32[]{:S(2)}) copy-start(bf16[1024,1024]{1,0:T(8,128)(2,1)} %constant.33.clone.dft_ref) | copy-start | bytes 6291460
  2.9 1.0 %copy-start.3 = (bf16[4,256,256]{2,1,0:T(8,128)(2,1)S(1)}, bf16[4,256,256]{2,1,0:T(8,128)(2,1)}, u32[]{:S(2)}) copy-start(bf16[4,256,256]{2,1,0:T(8,128)(2,1)} %constant.32.clone.fir_ref) | copy-start | bytes 1572868
  5.6 14.5 %collective-permute-start.1 = (bf16[128,1024]{1,0:T(8,128)(2,1)S(1)}, bf16[128,1024]{1,0:T(8,128)(2,1)S(1)}, u32[]{:S(2)}, u32[]{:S(2)}) collective-permute-start(bf16[128,1024]{1,0:T(8,128)(2,1)S(1)} %spectra.1.own_ref), channel_id=1, source_target_pairs={{0,248},{4,12},{8,0},{12,20},{16,8},{20,28},{24,16},{28,36},{32,24... | collective-permute-start | bytes 786440 | tf_op jit(solution)/shard_map/ppermute | solution.py:303
  13.7 7.2 %collective-permute-start.3 = (bf16[128,1024]{1,0:T(8,128)(2,1)S(1)}, bf16[128,1024]{1,0:T(8,128)(2,1)S(1)}, u32[]{:S(2)}, u32[]{:S(2)}) collective-permute-start(bf16[128,1024]{1,0:T(8,128)(2,1)S(1)} %spectra.1.own_ref), channel_id=1, source_target_pairs={{0,4},{4,0},{8,12},{12,8},{16,20},{20,16},{24,28},{28,24},{32,36},... | collective-permute-start | bytes 786440 | tf_op jit(solution)/shard_map/ppermute | solution.py:303
  13.7 9.7 %collective-permute-start = (bf16[128,1024]{1,0:T(8,128)(2,1)S(1)}, bf16[128,1024]{1,0:T(8,128)(2,1)S(1)}, u32[]{:S(2)}, u32[]{:S(2)}) collective-permute-start(bf16[128,1024]{1,0:T(8,128)(2,1)S(1)} %spectra.1.own_ref), channel_id=1, source_target_pairs={{0,8},{4,252},{8,16},{12,4},{16,24},{20,12},{24,32},{28,20},{32,40... | collective-permute-start | bytes 786440 | tf_op jit(solution)/shard_map/ppermute | solution.py:303
  20.2 3.3 %collective-permute-start.2 = (bf16[128,1024]{1,0:T(8,128)(2,1)S(1)}, bf16[128,1024]{1,0:T(8,128)(2,1)S(1)}, u32[]{:S(2)}, u32[]{:S(2)}) collective-permute-start(bf16[128,1024]{1,0:T(8,128)(2,1)S(1)} %collective-permute-done.1.far_ref), channel_id=1, source_target_pairs={{0,4},{4,0},{8,12},{12,8},{16,20},{20,16},{24,28},{28,24},{32,36},... | collective-permute-start | bytes 786440 | tf_op jit(solution)/shard_map/ppermute | solution.py:303
  20.9 9.9 %copy-start.4 = (s32[2,4,8]{2,1,0:T(4,128)S(1)}, s32[2,4,8]{2,1,0:T(4,128)}, u32[]{:S(2)}) copy-start(s32[2,4,8]{2,1,0:T(4,128)} %param.8) | copy-start | bytes 772
  20.9 9.9 %copy-start.5 = (s32[4]{0:T(128)S(1)}, s32[4]{0:T(128)}, u32[]{:S(2)}) copy-start(s32[4]{0:T(128)} %param.7) | copy-start | bytes 52
  20.9 19.6 %copy-start = (bf16[2,1024,512]{2,1,0:T(8,128)(2,1)S(1)}, bf16[2,1024,512]{2,1,0:T(8,128)(2,1)}, u32[]{:S(2)}) copy-start(bf16[2,1024,512]{2,1,0:T(8,128)(2,1)} %constant.34.clone.table_ref) | copy-start | bytes 6291460
  25.8 14.6 %all-to-all-start = ((bf16[4,96,1024]{2,1,0:T(8,128)(2,1)}), bf16[4,96,1024]{2,1,0:T(8,128)(2,1)S(1)}, u32[]{:S(2)}, u32[]{:S(2)}) async-start(bf16[4,96,1024]{2,1,0:T(8,128)(2,1)} %message.1), calls=%async_computation | async-start | bytes 1572864 | tf_op jit(solution)/shard_map/all_to_all | solution.py:313

commit v2 on v1

--- a/solution.py
+++ b/solution.py
@@ -25,7 +25,9 @@
 CANDS = 4
 MESSAGE = CANDS * PAIRS + 32
 VMEM = pltpu.MemorySpace.VMEM
+CHUNKS = 4
 LIMIT = 48 * 1024 * 1024
+WHOLE = 62 * 1024 * 1024
 bf16 = jnp.bfloat16
 f32 = jnp.float32
 
@@ -71,16 +73,43 @@
     return np.stack([high, low])
 
 
-def spectra_kernel(raw_ref, fir_ref, dft_ref, out_ref, wide_ref):
+def spectra_kernel(
+    raw_hbm, fir_hbm, dft_hbm, out_ref, raw_ref, fir_ref, dft_ref, wide_ref, sems
+):
+    def fetch(source, target, index):
+        return pltpu.make_async_copy(source, target, sems.at[index])
+
+    windows = raw_ref.shape[0] // CHUNKS
+    depth = LENGTH // CHUNKS
+    raw_copies = [
+        fetch(
+            raw_hbm.at[pl.ds(windows * c, windows)], raw_ref.at[pl.ds(windows * c, windows)], c
+        )
+        for c in range(CHUNKS)
+    ]
+    fir_copy = fetch(fir_hbm, fir_ref, CHUNKS)
+    dft_copies = [
+        fetch(
+            dft_hbm.at[pl.ds(depth * c, depth)],
+            dft_ref.at[pl.ds(depth * c, depth)],
+            CHUNKS + 1 + c,
+        )
+        for c in range(CHUNKS)
+    ]
+    for copy in raw_copies + [fir_copy] + dft_copies:
+        copy.start()
     blocks = LENGTH // LANE
     tail = raw_ref.shape[-1] - LENGTH
     wide_ref[blocks] = jnp.zeros((DEC * ROWS, LANE), f32)
-    for row in range(ROWS):
-        place = slice(row * DEC, (row + 1) * DEC)
-        values = raw_ref[row // SENSORS, row % SENSORS].astype(f32)
-        for k in range(blocks):
-            wide_ref[k, place] = values[:, LANE * k : LANE * (k + 1)]
-        wide_ref[blocks, place, :tail] = values[:, LENGTH:]
+    for c in range(CHUNKS):
+        raw_copies[c].wait()
+        for row in range(windows * SENSORS * c, windows * SENSORS * (c + 1)):
+            place = slice(row * DEC, (row + 1) * DEC)
+            values = raw_ref[row // SENSORS, row % SENSORS].astype(f32)
+            for k in range(blocks):
+                wide_ref[k, place] = values[:, LANE * k : LANE * (k + 1)]
+            wide_ref[blocks, place, :tail] = values[:, LENGTH:]
+    fir_copy.wait()
     total = jnp.zeros((SENSORS * ROWS, 2 * LANE), f32)
     for phase in range(DEC):
         samples = [
@@ -94,20 +123,31 @@
     decimated = jnp.concatenate(
         [summed[ROWS * k : ROWS * (k + 1)] for k in range(blocks)], axis=1
     )
-    out_ref[...] = jnp.dot(decimated, dft_ref[...], preferred_element_type=f32).astype(bf16)
+    for copy in dft_copies:
+        copy.wait()
+    spectra = jnp.dot(decimated, dft_ref[...], preferred_element_type=f32)
+    out_ref[...] = spectra.astype(bf16)
 
 
 def spectra_of(raw):
+    hbm = pl.BlockSpec(memory_space=pltpu.MemorySpace.HBM)
+    fir, dft = fir_table(), dft_table()
     return pl.pallas_call(
         spectra_kernel,
         out_shape=jax.ShapeDtypeStruct((ROWS, LENGTH), bf16),
-        in_specs=[pl.BlockSpec(memory_space=VMEM)] * 3,
+        in_specs=[hbm, hbm, hbm],
         out_specs=pl.BlockSpec(memory_space=VMEM),
-        scratch_shapes=[pltpu.VMEM((LENGTH // LANE + 1, DEC * ROWS, LANE), f32)],
-        compiler_params=pltpu.CompilerParams(vmem_limit_bytes=LIMIT),
+        scratch_shapes=[
+            pltpu.VMEM(raw.shape, bf16),
+            pltpu.VMEM(fir.shape, bf16),
+            pltpu.VMEM(dft.shape, bf16),
+            pltpu.VMEM((LENGTH // LANE + 1, DEC * ROWS, LANE), f32),
+            pltpu.SemaphoreType.DMA((2 * CHUNKS + 1,)),
+        ],
+        compiler_params=pltpu.CompilerParams(vmem_limit_bytes=WHOLE),
         cost_estimate=pl.CostEstimate(flops=2 * 10**9, bytes_accessed=5 * 10**6, transcendentals=0),
         name="spectra",
-    )(raw, jnp.asarray(fir_table()), jnp.asarray(dft_table()))
+    )(raw, jnp.asarray(fir), jnp.asarray(dft))
 
 
 def cross_body(own_ref, far_ref, store):
@@ -118,8 +158,8 @@
         def step(pair, totals):
             first, second, third, power = totals
             rows = pl.ds(pl.multiple_of(pair * 16, 16), 16)
-            own_real = own_ref[rows, real].astype(f32)
-            own_imag = own_ref[rows, imag].astype(f32)
+            own_real = own_ref[rows, real]
+            own_imag = own_ref[rows, imag]
             far_real = far_ref[rows, real].astype(f32)
             far_imag = far_ref[rows, imag].astype(f32)
             own_sum = own_real + own_imag
@@ -143,18 +183,18 @@
         store(real, imag, first, second, third, power)
 
 
-def put_cross(out_ref, base, real, imag, first, second, third):
-    for y in range(4):
-        pair = [2 * y, 2 * y + 1]
+def put_cross(out_refs, base, real, imag, first, second, third):
+    for k in range(4):
+        pair = [2 * k, 2 * k + 1]
         real_cross = jnp.concatenate([first[i] + second[i] for i in pair], axis=0)
         imag_cross = jnp.concatenate([third[i] - first[i] + second[i] for i in pair], axis=0)
-        out_ref[y, base : base + PAIRS, real] = real_cross.astype(bf16)
-        out_ref[y, base : base + PAIRS, imag] = imag_cross.astype(bf16)
+        out_refs[k][base : base + PAIRS, real] = real_cross.astype(bf16)
+        out_refs[k][base : base + PAIRS, imag] = imag_cross.astype(bf16)
 
 
 def cross_kernel(own_ref, far_ref, out_ref, power_ref):
     def store(real, imag, first, second, third, power):
-        put_cross(out_ref, 0, real, imag, first, second, third)
+        put_cross([out_ref.at[k] for k in range(4)], 0, real, imag, first, second, third)
         power_ref[:, real] = power
 
     cross_body(own_ref, far_ref, store)
@@ -175,23 +215,46 @@
     )(own, far)
 
 
-def message_kernel(own_ref, third_ref, fourth_ref, s_ref, sp_ref, a_ref, ap_ref, out_ref):
-    for y in range(4):
-        out_ref[y, 0:PAIRS] = s_ref[y]
-        out_ref[y, PAIRS : 2 * PAIRS] = a_ref[y]
-    base = CANDS * PAIRS
-    own_power = jnp.zeros((SENSORS, BINS), f32)
-    for w in range(WIN // 2):
-        block = own_ref[16 * w : 16 * (w + 1)].astype(f32)
+def own_kernel(turn_ref, spectra_ref, own_ref, mine_ref):
+    shift = lax.rem(SENSORS - 2 * turn_ref[0], SENSORS)
+    power = jnp.zeros((SENSORS, BINS), f32)
+    for window in range(WIN):
+        rows = slice(SENSORS * window, SENSORS * (window + 1))
+        block = pltpu.roll(spectra_ref[rows].astype(f32), shift, 0)
+        own_ref[rows] = block
         square = block * block
-        square = square[:SENSORS] + square[SENSORS:]
-        own_power = own_power + (square[:, :BINS] + square[:, BINS:])
+        power = power + (square[:, :BINS] + square[:, BINS:])
+    high = power.astype(bf16).astype(f32)
+    mine = jnp.concatenate([high, power - high], axis=1)
+    for k in range(4):
+        mine_ref[k] = jnp.concatenate([mine[2 * k : 2 * k + 2]] * SENSORS, axis=0).astype(bf16)
+
+
+def own_of(turn, spectra):
+    vmem = pl.BlockSpec(memory_space=VMEM)
+    return pl.pallas_call(
+        own_kernel,
+        out_shape=(
+            jax.ShapeDtypeStruct((ROWS, LENGTH), f32),
+            jax.ShapeDtypeStruct((4, 16, LENGTH), bf16),
+        ),
+        in_specs=[pl.BlockSpec(memory_space=pltpu.MemorySpace.SMEM), vmem],
+        out_specs=(vmem, vmem),
+        compiler_params=pltpu.CompilerParams(vmem_limit_bytes=LIMIT),
+        cost_estimate=pl.CostEstimate(flops=10**6, bytes_accessed=10**6, transcendentals=0),
+        name="own",
+    )(turn, spectra)
+
+
+def message_kernel(
+    own_ref, third_ref, fourth_ref, s_ref, sp_ref, a_ref, ap_ref, mine_ref, *out_refs
+):
     powers = {0: sp_ref[...], 1: ap_ref[...]}
     for slot, far_ref in ((2, third_ref), (3, fourth_ref)):
         collected = []
 
         def store(real, imag, first, second, third, power):
-            put_cross(out_ref, slot * PAIRS, real, imag, first, second, third)
+            put_cross(out_refs, slot * PAIRS, real, imag, first, second, third)
             collected.append(power)
 
         cross_body(own_ref, far_ref, store)
@@ -203,46 +266,42 @@
         ],
         axis=0,
     ).astype(bf16)
-    high = own_power.astype(bf16)
-    low = (own_power - high.astype(f32)).astype(bf16)
-    mine = jnp.concatenate([high, low], axis=1)
-    mine = jnp.concatenate([mine, mine], axis=0)
-    for y in range(4):
-        out_ref[y, base : base + 16] = near
-        out_ref[y, base + 16 : base + 32] = mine
-
-
-def message_of(own, third, fourth, s_cross, s_power, a_cross, a_power):
+    base = CANDS * PAIRS
+    for k in range(4):
+        out_refs[k][0:PAIRS] = s_ref[k]
+        out_refs[k][PAIRS : 2 * PAIRS] = a_ref[k]
+        out_refs[k][base : base + 16] = near
+        out_refs[k][base + 16 : base + 32] = mine_ref[k]
+
+
+def messages_of(*parts):
+    vmem = pl.BlockSpec(memory_space=VMEM)
     return pl.pallas_call(
         message_kernel,
-        out_shape=jax.ShapeDtypeStruct((4, MESSAGE, LENGTH), bf16),
-        in_specs=[pl.BlockSpec(memory_space=VMEM)] * 7,
-        out_specs=pl.BlockSpec(memory_space=VMEM),
+        out_shape=(jax.ShapeDtypeStruct((MESSAGE, LENGTH), bf16),) * 4,
+        in_specs=[vmem] * 8,
+        out_specs=(vmem,) * 4,
         compiler_params=pltpu.CompilerParams(vmem_limit_bytes=LIMIT),
         cost_estimate=pl.CostEstimate(flops=2 * 10**8, bytes_accessed=10**6, transcendentals=0),
         name="message",
-    )(own, third, fourth, s_cross, s_power, a_cross, a_power)
-
-
-def lag_kernel(slots_ref, position_ref, got_ref, table_ref, mask_ref, out_ref, lagged_ref):
+    )(*parts)
+
+
+def lag_kernel(slots_ref, table_ref, mask_ref, *refs):
+    got_refs, out_ref, lagged_ref = refs[:4], refs[4], refs[5]
     base = CANDS * PAIRS
 
     def summed(rows):
-        return (got_ref[0, rows].astype(f32) + got_ref[1, rows].astype(f32)) + (
-            got_ref[2, rows].astype(f32) + got_ref[3, rows].astype(f32)
-        )
+        parts = [ref[rows].astype(f32) for ref in got_refs]
+        return (parts[0] + parts[1]) + (parts[2] + parts[3])
 
     def inverse(power):
         return lax.rsqrt(power / (4 * WIN) + 1e-06 * SCALE * SCALE)
 
     near = inverse(summed(slice(base, base + 16)))
-    mine = summed(slice(base + 16, base + 32))[:SENSORS]
+    mine = summed(slice(base + 16, base + 32))
     mine = inverse(mine[:, :BINS] + mine[:, BINS:])
-    y = position_ref[0]
-    sensor = lax.broadcasted_iota(jnp.int32, (SENSORS, BINS), 0)
-    own = [
-        jnp.sum(jnp.where(sensor == 2 * y + i, mine, 0.0), axis=0, keepdims=True) for i in range(2)
-    ]
+    own = [mine[i : i + 1] for i in range(2)]
     pieces = []
     for slot in range(CANDS):
         row, column = slot // 2, slot % 2
@@ -255,9 +314,10 @@
     whitened = jnp.concatenate(pieces, axis=0)
     high = whitened.astype(bf16)
     low = (whitened - high.astype(f32)).astype(bf16)
-    lagged = jnp.dot(high, table_ref[0], preferred_element_type=f32)
+    both = jnp.concatenate([high, low], axis=0)
+    lagged = jnp.dot(both, table_ref[0], preferred_element_type=f32)
+    lagged = lagged[: CANDS * PAIRS] + lagged[CANDS * PAIRS :]
     lagged = lagged + jnp.dot(high, table_ref[1], preferred_element_type=f32)
-    lagged = lagged + jnp.dot(low, table_ref[0], preferred_element_type=f32)
     lagged_ref[...] = lagged.reshape(CANDS, 2, SENSORS, LAGS)
     normaliser = 1.0 / math.sqrt(4 * WIN * BINS)
     for r in range(4):
@@ -269,19 +329,19 @@
                 out_ref[i, r, :, lanes] = lagged_ref[slot, i, :, lanes] * factor
 
 
-def lag_of(slots, position, got, mask):
+def lag_of(slots, mask, *got):
     smem = pl.BlockSpec(memory_space=pltpu.MemorySpace.SMEM)
     vmem = pl.BlockSpec(memory_space=VMEM)
     return pl.pallas_call(
         lag_kernel,
         out_shape=jax.ShapeDtypeStruct((2, 4, SENSORS, LAGS), f32),
-        in_specs=[smem, smem, vmem, vmem, vmem],
+        in_specs=[smem] + [vmem] * 6,
         out_specs=vmem,
         scratch_shapes=[pltpu.VMEM((CANDS, 2, SENSORS, LAGS), f32)],
         compiler_params=pltpu.CompilerParams(vmem_limit_bytes=LIMIT),
         cost_estimate=pl.CostEstimate(flops=2 * 10**8, bytes_accessed=3 * 10**6, transcendentals=0),
         name="lag",
-    )(slots, position, got, jnp.asarray(lag_table()), mask)
+    )(slots, jnp.asarray(lag_table()), mask, *got)
 
 
 def per_device(raw, blocks, mask):
@@ -295,23 +355,30 @@
         0,
         jnp.where(relative == -other, 3, jnp.where(relative == 2 * other, 1, 2)),
     ).astype(jnp.int32)
-    position = lax.axis_index("tm").astype(jnp.int32).reshape(1)
+    turn = lax.axis_index("tm").astype(jnp.int32).reshape(1)
     wide_mask = jnp.broadcast_to(mask.astype(f32)[..., None], mask.shape + (LANE,))
 
     def ring(block, distances):
         route = [(i, (i + distances[i % 2]) % tiles) for i in range(tiles)]
         return lax.ppermute(block, "tile", route)
+
+    def onward(block, distance):
+        groups = lax.axis_size("tm")
+        return lax.ppermute(block, "tm", [(i, (i + distance) % groups) for i in range(groups)])
 
     spectra = spectra_of(raw)
     near = ring(spectra, (1, -1))
     ahead = ring(spectra, (-2, 2))
     behind = ring(spectra, (2, -2))
     corner = ring(ahead, (1, -1))
-    s_cross, s_power = cross_of(spectra, near)
-    a_cross, a_power = cross_of(spectra, ahead)
-    message = message_of(spectra, behind, corner, s_cross, s_power, a_cross, a_power)
-    got = lax.all_to_all(message, "tm", 0, 0)
-    return lag_of(slots, position, got, wide_mask)
+    own, mine = own_of(turn, spectra)
+    s_cross, s_power = cross_of(own, near)
+    a_cross, a_power = cross_of(own, ahead)
+    messages = messages_of(
+        own, behind, corner, s_cross, s_power, a_cross, a_power, mine
+    )
+    got = [messages[0]] + [onward(messages[k], k) for k in (2, 1, 3)]
+    return lag_of(slots, wide_mask, *got)
 
 
 def solution(mesh):

time: 42.7 us -> 38.6 us (0.904)
  the two profiles are of different devices: /device:TPU:8 before, /device:TPU:1 now
where the time goes in v2:
time: 38.6 us; the launch traced here: 38.4 us
  starting transfers between devices  19.6 us (51%)
  waiting for transfers between devices  9.09 us (24%)
  Pallas kernels  8.68 us (22%)
  local copies, waits for them, and re-layouts  1.04 us (3%)
    ppermute x4, starting transfers between devices, ring(): return lax.ppermute(block, 'tile', route)  13.9 us
    ppermute x3, waiting for transfers between devices, onward(): lax.ppermute(block, 'tm', [(i, (i + distance) % groups) for i in range(gr...  6.61 us
    ppermute x3, starting transfers between devices, onward(): lax.ppermute(block, 'tm', [(i, (i + distance) % groups) for i in range(gr...  5.67 us
    pallas_call x1, Pallas kernels, spectra_of(): pl.pallas_call(spectra_kernel, out_shape=jax.ShapeDtypeStruct((ROWS, LENG...  3.87 us
    ppermute x4, waiting for transfers between devices, ring(): return lax.ppermute(block, 'tile', route)  2.48 us
    pallas_call x1, Pallas kernels, lag_of(): pl.pallas_call(lag_kernel, out_shape=jax.ShapeDtypeStruct((2, 4, SENSORS,...  1.7 us
    pallas_call x1, Pallas kernels, messages_of(): pl.pallas_call(message_kernel, out_shape=(jax.ShapeDtypeStruct((MESSAGE,...  1.52 us
    pallas_call x2, Pallas kernels, cross_of(): pl.pallas_call(cross_kernel, out_shape=(jax.ShapeDtypeStruct((4, PAIRS, L...  1.49 us
  transfers between devices with their start and end apart: 7, of which 3 were waited for; matrix products, arithmetic and copies ran while one was open for 0% of the time, Pallas kernels for 4%

profile of v2, /device:TPU:1, one launch (start us, length us, event | category | flops | bytes accessed | tf_op | source)
XLA Modules:
  0.0 38.4 jit_solution(15337254385521658679)
XLA Ops:
  0.0 3.9 %spectra.1.spectra_ref = bf16[128,1024]{1,0:T(8,128)(2,1)} custom-call(bf16[16,8,4,1039]{3,2,1,0:T(4,128)(2,1)} %raw_hbm.1, bf16[4,256,256]{2,1,0:T(8,128)(2,1)} %constant.32.clone.fir_hbm, bf16[1024,1024]{1,0:T(8,128)(2,1)} %constant.33.clone.dft_hbm), custom_call_target="tpu_custom_call" | custom-call | flops 2000000000 | bytes 5000000 | tf_op jit(solution)/shard_map/spectra/pallas_call | solution.py:135
  3.9 0.0 copy-start
  3.9 2.1 %collective-permute-start.1 = (bf16[128,1024]{1,0:T(8,128)(2,1)}, bf16[128,1024]{1,0:T(8,128)(2,1)S(1)}, u32[]{:S(2)}, u32[]{:S(2)}) collective-permute-start(bf16[128,1024]{1,0:T(8,128)(2,1)} %spectra.1.spectra_ref), channel_id=1, source_target_pairs={{0,248},{4,12},{8,0},{12,20},{16,8},{20,28},{24,16},{28,36},{32,24... | collective-permute-start | bytes 786440 | tf_op jit(solution)/shard_map/ppermute | solution.py:363
  6.0 7.5 %collective-permute-start.3 = (bf16[128,1024]{1,0:T(8,128)(2,1)}, bf16[128,1024]{1,0:T(8,128)(2,1)S(1)}, u32[]{:S(2)}, u32[]{:S(2)}) collective-permute-start(bf16[128,1024]{1,0:T(8,128)(2,1)} %spectra.1.spectra_ref), channel_id=1, source_target_pairs={{0,4},{4,0},{8,12},{12,8},{16,20},{20,16},{24,28},{28,24},{32,36},... | collective-permute-start | bytes 786440 | tf_op jit(solution)/shard_map/ppermute | solution.py:363
  13.5 0.5 %collective-permute-start = (bf16[128,1024]{1,0:T(8,128)(2,1)}, bf16[128,1024]{1,0:T(8,128)(2,1)S(1)}, u32[]{:S(2)}, u32[]{:S(2)}) collective-permute-start(bf16[128,1024]{1,0:T(8,128)(2,1)} %spectra.1.spectra_ref), channel_id=1, source_target_pairs={{0,8},{4,252},{8,16},{12,4},{16,24},{20,12},{24,32},{28,20},{32,40... | collective-permute-start | bytes 786440 | tf_op jit(solution)/shard_map/ppermute | solution.py:363
  14.1 2.5 %collective-permute-done.1.far_ref = bf16[128,1024]{1,0:T(8,128)(2,1)S(1)} collective-permute-done((bf16[128,1024]{1,0:T(8,128)(2,1)}, bf16[128,1024]{1,0:T(8,128)(2,1)S(1)}, u32[]{:S(2)}, u32[]{:S(2)}) %collective-permute-start.1) | collective-permute-done | bytes 262176 | tf_op jit(solution)/shard_map/ppermute | solution.py:363
  16.5 3.7 %collective-permute-start.2 = (bf16[128,1024]{1,0:T(8,128)(2,1)S(1)}, bf16[128,1024]{1,0:T(8,128)(2,1)S(1)}, u32[]{:S(2)}, u32[]{:S(2)}) collective-permute-start(bf16[128,1024]{1,0:T(8,128)(2,1)S(1)} %collective-permute-done.1.far_ref), channel_id=1, source_target_pairs={{0,4},{4,0},{8,12},{12,8},{16,20},{20,16},{24,28},{28,24},{32,36},... | collective-permute-start | bytes 786440 | tf_op jit(solution)/shard_map/ppermute | solution.py:363
  20.3 0.9 %copy-done.1 = bf16[128,1024]{1,0:T(8,128)(2,1)S(1)} copy-done((bf16[128,1024]{1,0:T(8,128)(2,1)S(1)}, bf16[128,1024]{1,0:T(8,128)(2,1)}, u32[]{:S(2)}) %copy-start.1) | copy-done | bytes 262168
  21.2 0.1 own.1
  21.3 0.7 %cross.3 = (bf16[4,16,1024]{2,1,0:T(8,128)(2,1)S(1)}, f32[8,512]{1,0:T(8,128)S(1)}) custom-call(f32[128,1024]{1,0:T(8,128)S(1)} %get-tuple-element.15.own_ref, bf16[128,1024]{1,0:T(8,128)(2,1)S(1)} %collective-permute-done.1.far_ref), custom_call_target="tpu_custom_call" | custom-call | flops 100000000 | bytes 1000000 | tf_op jit(solution)/shard_map/cross/pallas_call | solution.py:204
  22.1 0.0 collective-permute-done.3.far_ref
  22.1 0.7 %cross.2 = (bf16[4,16,1024]{2,1,0:T(8,128)(2,1)S(1)}, f32[8,512]{1,0:T(8,128)S(1)}) custom-call(f32[128,1024]{1,0:T(8,128)S(1)} %get-tuple-element.15.own_ref, bf16[128,1024]{1,0:T(8,128)(2,1)S(1)} %collective-permute-done.3.far_ref), custom_call_target="tpu_custom_call" | custom-call | flops 100000000 | bytes 1000000 | tf_op jit(solution)/shard_map/cross/pallas_call | solution.py:204
  22.8 0.0 collective-permute-done.third_ref
  22.8 0.0 collective-permute-done.2.fourth_ref
  22.9 1.5 %message.1 = (bf16[96,1024]{1,0:T(8,128)(2,1)S(1)}, bf16[96,1024]{1,0:T(8,128)(2,1)S(1)}, bf16[96,1024]{1,0:T(8,128)(2,1)S(1)}, bf16[96,1024]{1,0:T(8,128)(2,1)S(1)}) custom-call(f32[128,1024]{1,0:T(8,128)S(1)} %get-tuple-element.15.own_ref, bf16[128,1024]{1,0:T(8,128)(2,1)S(1)} %collective-permute-done.third_ref, ...), custom_call_target="tpu_custom_call" | custom-call | flops 200000000 | bytes 1000000 | tf_op jit(solution)/shard_map/message/pallas_call | solution.py:279
  24.4 3.0 %collective-permute-start.4 = (bf16[96,1024]{1,0:T(8,128)(2,1)S(1)}, bf16[96,1024]{1,0:T(8,128)(2,1)S(1)}, u32[]{:S(2)}, u32[]{:S(2)}) collective-permute-start(bf16[96,1024]{1,0:T(8,128)(2,1)S(1)} %get-tuple-element.22), channel_id=1, source_target_pairs={{0,2},{1,3},{2,0},{3,1},{4,6},{5,7},{6,4},{7,5},{8,10},{9,11},{10,... | collective-permute-start | bytes 589832 | tf_op jit(solution)/shard_map/ppermute | solution.py:367
  27.4 0.4 %collective-permute-start.5 = (bf16[96,1024]{1,0:T(8,128)(2,1)S(1)}, bf16[96,1024]{1,0:T(8,128)(2,1)S(1)}, u32[]{:S(2)}, u32[]{:S(2)}) collective-permute-start(bf16[96,1024]{1,0:T(8,128)(2,1)S(1)} %get-tuple-element.23), channel_id=1, source_target_pairs={{0,1},{1,2},{2,3},{3,0},{4,5},{5,6},{6,7},{7,4},{8,9},{9,10},{10,1... | collective-permute-start | bytes 589832 | tf_op jit(solution)/shard_map/ppermute | solution.py:367
  27.8 2.3 %collective-permute-start.6 = (bf16[96,1024]{1,0:T(8,128)(2,1)S(1)}, bf16[96,1024]{1,0:T(8,128)(2,1)S(1)}, u32[]{:S(2)}, u32[]{:S(2)}) collective-permute-start(bf16[96,1024]{1,0:T(8,128)(2,1)S(1)} %get-tuple-element.24), channel_id=1, source_target_pairs={{0,3},{1,0},{2,1},{3,2},{4,7},{5,4},{6,5},{7,6},{8,11},{9,8},{10,9... | collective-permute-start | bytes 589832 | tf_op jit(solution)/shard_map/ppermute | solution.py:367
  30.0 0.0 copy-done.3
  30.1 1.8 %collective-permute-done.4.refs_1_ = bf16[96,1024]{1,0:T(8,128)(2,1)S(1)} collective-permute-done((bf16[96,1024]{1,0:T(8,128)(2,1)S(1)}, bf16[96,1024]{1,0:T(8,128)(2,1)S(1)}, u32[]{:S(2)}, u32[]{:S(2)}) %collective-permute-start.4) | collective-permute-done | bytes 196640 | tf_op jit(solution)/shard_map/ppermute | solution.py:367
  31.8 4.8 %collective-permute-done.5.refs_2_ = bf16[96,1024]{1,0:T(8,128)(2,1)S(1)} collective-permute-done((bf16[96,1024]{1,0:T(8,128)(2,1)S(1)}, bf16[96,1024]{1,0:T(8,128)(2,1)S(1)}, u32[]{:S(2)}, u32[]{:S(2)}) %collective-permute-start.5) | collective-permute-done | bytes 196640 | tf_op jit(solution)/shard_map/ppermute | solution.py:367
  36.7 0.0 collective-permute-done.6.refs_3_
  36.7 0.1 broadcast_in_dim.25.mask_ref
  36.7 1.7 %lag.1 = f32[2,4,8,512]{3,2,1,0:T(8,128)} custom-call(s32[4]{0:T(128)S(1)} %compare_select_fusion.2.slots_ref, bf16[2,1024,512]{2,1,0:T(8,128)(2,1)S(1)} %copy-done, f32[2,4,8,128]{3,2,1,0:T(8,128)S(1)} %broadcast_in_dim.25.mask_ref, bf16[96,1024]{1,0:T(8,128)(2,1)S(1)} %get-tuple-element.21.refs_0_, bf16[96,1024]{1,0:T(8,128)(2,1)S(1)} %collective-permute-done.4.refs_1_, ...), custom_call_target="tpu_custom_call" | custom-call | flops 200000000 | bytes 3000000 | tf_op jit(solution)/shard_map/lag/pallas_call | solution.py:335
  (7 shorter events, 0.0 us)
Async XLA Ops:
  0.0 20.3 %copy-start.2 = (s32[2,4,8]{2,1,0:T(4,128)S(1)}, s32[2,4,8]{2,1,0:T(4,128)}, u32[]{:S(2)}) copy-start(s32[2,4,8]{2,1,0:T(4,128)} %param.8) | copy-start | bytes 772
  0.0 30.0 %copy-start.3 = (s32[4]{0:T(128)S(1)}, s32[4]{0:T(128)}, u32[]{:S(2)}) copy-start(s32[4]{0:T(128)} %param.7) | copy-start | bytes 52
  3.9 32.9 %copy-start = (bf16[2,1024,512]{2,1,0:T(8,128)(2,1)S(1)}, bf16[2,1024,512]{2,1,0:T(8,128)(2,1)}, u32[]{:S(2)}) copy-start(bf16[2,1024,512]{2,1,0:T(8,128)(2,1)} %constant.34.clone.table_ref) | copy-start | bytes 6291460
  3.9 12.7 %collective-permute-start.1 = (bf16[128,1024]{1,0:T(8,128)(2,1)}, bf16[128,1024]{1,0:T(8,128)(2,1)S(1)}, u32[]{:S(2)}, u32[]{:S(2)}) collective-permute-start(bf16[128,1024]{1,0:T(8,128)(2,1)} %spectra.1.spectra_ref), channel_id=1, source_target_pairs={{0,248},{4,12},{8,0},{12,20},{16,8},{20,28},{24,16},{28,36},{32,24... | collective-permute-start | bytes 786440 | tf_op jit(solution)/shard_map/ppermute | solution.py:363
  6.0 16.1 %collective-permute-start.3 = (bf16[128,1024]{1,0:T(8,128)(2,1)}, bf16[128,1024]{1,0:T(8,128)(2,1)S(1)}, u32[]{:S(2)}, u32[]{:S(2)}) collective-permute-start(bf16[128,1024]{1,0:T(8,128)(2,1)} %spectra.1.spectra_ref), channel_id=1, source_target_pairs={{0,4},{4,0},{8,12},{12,8},{16,20},{20,16},{24,28},{28,24},{32,36},... | collective-permute-start | bytes 786440 | tf_op jit(solution)/shard_map/ppermute | solution.py:363
  13.5 9.3 %collective-permute-start = (bf16[128,1024]{1,0:T(8,128)(2,1)}, bf16[128,1024]{1,0:T(8,128)(2,1)S(1)}, u32[]{:S(2)}, u32[]{:S(2)}) collective-permute-start(bf16[128,1024]{1,0:T(8,128)(2,1)} %spectra.1.spectra_ref), channel_id=1, source_target_pairs={{0,8},{4,252},{8,16},{12,4},{16,24},{20,12},{24,32},{28,20},{32,40... | collective-permute-start | bytes 786440 | tf_op jit(solution)/shard_map/ppermute | solution.py:363
  16.5 6.3 %collective-permute-start.2 = (bf16[128,1024]{1,0:T(8,128)(2,1)S(1)}, bf16[128,1024]{1,0:T(8,128)(2,1)S(1)}, u32[]{:S(2)}, u32[]{:S(2)}) collective-permute-start(bf16[128,1024]{1,0:T(8,128)(2,1)S(1)} %collective-permute-done.1.far_ref), channel_id=1, source_target_pairs={{0,4},{4,0},{8,12},{12,8},{16,20},{20,16},{24,28},{28,24},{32,36},... | collective-permute-start | bytes 786440 | tf_op jit(solution)/shard_map/ppermute | solution.py:363
  20.3 1.0 %copy-start.1 = (bf16[128,1024]{1,0:T(8,128)(2,1)S(1)}, bf16[128,1024]{1,0:T(8,128)(2,1)}, u32[]{:S(2)}) copy-start(bf16[128,1024]{1,0:T(8,128)(2,1)} %spectra.1.spectra_ref) | copy-start | bytes 786436
  24.4 7.5 %collective-permute-start.4 = (bf16[96,1024]{1,0:T(8,128)(2,1)S(1)}, bf16[96,1024]{1,0:T(8,128)(2,1)S(1)}, u32[]{:S(2)}, u32[]{:S(2)}) collective-permute-start(bf16[96,1024]{1,0:T(8,128)(2,1)S(1)} %get-tuple-element.22), channel_id=1, source_target_pairs={{0,2},{1,3},{2,0},{3,1},{4,6},{5,7},{6,4},{7,5},{8,10},{9,11},{10,... | collective-permute-start | bytes 589832 | tf_op jit(solution)/shard_map/ppermute | solution.py:367
  27.4 9.3 %collective-permute-start.5 = (bf16[96,1024]{1,0:T(8,128)(2,1)S(1)}, bf16[96,1024]{1,0:T(8,128)(2,1)S(1)}, u32[]{:S(2)}, u32[]{:S(2)}) collective-permute-start(bf16[96,1024]{1,0:T(8,128)(2,1)S(1)} %get-tuple-element.23), channel_id=1, source_target_pairs={{0,1},{1,2},{2,3},{3,0},{4,5},{5,6},{6,7},{7,4},{8,9},{9,10},{10,1... | collective-permute-start | bytes 589832 | tf_op jit(solution)/shard_map/ppermute | solution.py:367
  27.8 8.9 %collective-permute-start.6 = (bf16[96,1024]{1,0:T(8,128)(2,1)S(1)}, bf16[96,1024]{1,0:T(8,128)(2,1)S(1)}, u32[]{:S(2)}, u32[]{:S(2)}) collective-permute-start(bf16[96,1024]{1,0:T(8,128)(2,1)S(1)} %get-tuple-element.24), channel_id=1, source_target_pairs={{0,3},{1,0},{2,1},{3,2},{4,7},{5,4},{6,5},{7,6},{8,11},{9,8},{10,9... | collective-permute-start | bytes 589832 | tf_op jit(solution)/shard_map/ppermute | solution.py:367

commit v3 on v2

--- a/solution.py
+++ b/solution.py
@@ -26,8 +26,8 @@
 MESSAGE = CANDS * PAIRS + 32
 VMEM = pltpu.MemorySpace.VMEM
 CHUNKS = 4
-LIMIT = 48 * 1024 * 1024
-WHOLE = 62 * 1024 * 1024
+LAG_PASSES = 2
+LIMIT = 16 * 1024 * 1024
 bf16 = jnp.bfloat16
 f32 = jnp.float32
 
@@ -129,12 +129,16 @@
     out_ref[...] = spectra.astype(bf16)
 
 
+def in_hbm(array):
+    return pltpu.with_memory_space_constraint(array, pltpu.MemorySpace.HBM)
+
+
 def spectra_of(raw):
     hbm = pl.BlockSpec(memory_space=pltpu.MemorySpace.HBM)
     fir, dft = fir_table(), dft_table()
     return pl.pallas_call(
         spectra_kernel,
-        out_shape=jax.ShapeDtypeStruct((ROWS, LENGTH), bf16),
+        out_shape=pltpu.VMEM((ROWS, LENGTH), bf16),
         in_specs=[hbm, hbm, hbm],
         out_specs=pl.BlockSpec(memory_space=VMEM),
         scratch_shapes=[
@@ -144,10 +148,10 @@
             pltpu.VMEM((LENGTH // LANE + 1, DEC * ROWS, LANE), f32),
             pltpu.SemaphoreType.DMA((2 * CHUNKS + 1,)),
         ],
-        compiler_params=pltpu.CompilerParams(vmem_limit_bytes=WHOLE),
-        cost_estimate=pl.CostEstimate(flops=2 * 10**9, bytes_accessed=5 * 10**6, transcendentals=0),
+        compiler_params=pltpu.CompilerParams(vmem_limit_bytes=LIMIT),
+        cost_estimate=pl.CostEstimate(flops=10**5, bytes_accessed=10**4, transcendentals=0),
         name="spectra",
-    )(raw, jnp.asarray(fir), jnp.asarray(dft))
+    )(in_hbm(raw), in_hbm(jnp.asarray(fir)), in_hbm(jnp.asarray(dft)))
 
 
 def cross_body(own_ref, far_ref, store):
@@ -204,13 +208,13 @@
     return pl.pallas_call(
         cross_kernel,
         out_shape=(
-            jax.ShapeDtypeStruct((4, PAIRS, LENGTH), bf16),
-            jax.ShapeDtypeStruct((SENSORS, BINS), f32),
+            pltpu.VMEM((4, PAIRS, LENGTH), bf16),
+            pltpu.VMEM((SENSORS, BINS), f32),
         ),
         in_specs=[pl.BlockSpec(memory_space=VMEM)] * 2,
         out_specs=(pl.BlockSpec(memory_space=VMEM),) * 2,
         compiler_params=pltpu.CompilerParams(vmem_limit_bytes=LIMIT),
-        cost_estimate=pl.CostEstimate(flops=10**8, bytes_accessed=10**6, transcendentals=0),
+        cost_estimate=pl.CostEstimate(flops=10**5, bytes_accessed=10**4, transcendentals=0),
         name="cross",
     )(own, far)
 
@@ -235,13 +239,13 @@
     return pl.pallas_call(
         own_kernel,
         out_shape=(
-            jax.ShapeDtypeStruct((ROWS, LENGTH), f32),
-            jax.ShapeDtypeStruct((4, 16, LENGTH), bf16),
+            pltpu.VMEM((ROWS, LENGTH), f32),
+            pltpu.VMEM((4, 16, LENGTH), bf16),
         ),
         in_specs=[pl.BlockSpec(memory_space=pltpu.MemorySpace.SMEM), vmem],
         out_specs=(vmem, vmem),
         compiler_params=pltpu.CompilerParams(vmem_limit_bytes=LIMIT),
-        cost_estimate=pl.CostEstimate(flops=10**6, bytes_accessed=10**6, transcendentals=0),
+        cost_estimate=pl.CostEstimate(flops=10**5, bytes_accessed=10**4, transcendentals=0),
         name="own",
     )(turn, spectra)
 
@@ -278,16 +282,16 @@
     vmem = pl.BlockSpec(memory_space=VMEM)
     return pl.pallas_call(
         message_kernel,
-        out_shape=(jax.ShapeDtypeStruct((MESSAGE, LENGTH), bf16),) * 4,
+        out_shape=(pltpu.VMEM((MESSAGE, LENGTH), bf16),) * 4,
         in_specs=[vmem] * 8,
         out_specs=(vmem,) * 4,
         compiler_params=pltpu.CompilerParams(vmem_limit_bytes=LIMIT),
-        cost_estimate=pl.CostEstimate(flops=2 * 10**8, bytes_accessed=10**6, transcendentals=0),
+        cost_estimate=pl.CostEstimate(flops=10**5, bytes_accessed=10**4, transcendentals=0),
         name="message",
     )(*parts)
 
 
-def lag_kernel(slots_ref, table_ref, mask_ref, *refs):
+def lag_kernel(tile_ref, blocks_ref, mask_ref, table_ref, *refs):
     got_refs, out_ref, lagged_ref = refs[:4], refs[4], refs[5]
     base = CANDS * PAIRS
 
@@ -313,50 +317,55 @@
             pieces.append(cross[SENSORS * i : SENSORS * (i + 1)] * factor)
     whitened = jnp.concatenate(pieces, axis=0)
     high = whitened.astype(bf16)
-    low = (whitened - high.astype(f32)).astype(bf16)
-    both = jnp.concatenate([high, low], axis=0)
-    lagged = jnp.dot(both, table_ref[0], preferred_element_type=f32)
-    lagged = lagged[: CANDS * PAIRS] + lagged[CANDS * PAIRS :]
-    lagged = lagged + jnp.dot(high, table_ref[1], preferred_element_type=f32)
+    if LAG_PASSES == 1:
+        lagged = jnp.dot(high, table_ref[0], preferred_element_type=f32)
+    else:
+        low = (whitened - high.astype(f32)).astype(bf16)
+        both = jnp.concatenate([high, low], axis=0)
+        lagged = jnp.dot(both, table_ref[0], preferred_element_type=f32)
+        lagged = lagged[: CANDS * PAIRS] + lagged[CANDS * PAIRS :]
+        if LAG_PASSES == 3:
+            lagged = lagged + jnp.dot(high, table_ref[1], preferred_element_type=f32)
     lagged_ref[...] = lagged.reshape(CANDS, 2, SENSORS, LAGS)
     normaliser = 1.0 / math.sqrt(4 * WIN * BINS)
+    tile = tile_ref[0]
+    other = 1 - 2 * lax.rem(tile, 2)
+    diagonal = lax.broadcasted_iota(jnp.int32, (SENSORS, SENSORS), 0) == (
+        lax.broadcasted_iota(jnp.int32, (SENSORS, SENSORS), 1)
+    )
     for r in range(4):
-        slot = slots_ref[r]
+        relative = blocks_ref[r] - tile
+        slot = jnp.where(
+            relative == other,
+            0,
+            jnp.where(relative == -other, 3, jnp.where(relative == 2 * other, 1, 2)),
+        )
         for i in range(2):
-            factor = mask_ref[i, r] * normaliser
-            for k in range(LAGS // LANE):
-                lanes = slice(LANE * k, LANE * (k + 1))
-                out_ref[i, r, :, lanes] = lagged_ref[slot, i, :, lanes] * factor
-
-
-def lag_of(slots, mask, *got):
+            row = mask_ref[i, r : r + 1, :].astype(f32) * normaliser
+            column = jnp.sum(jnp.where(diagonal, row, 0.0), axis=1, keepdims=True)
+            out_ref[i, r] = lagged_ref[slot, i] * column
+
+
+def lag_of(tile, blocks, mask, *got):
     smem = pl.BlockSpec(memory_space=pltpu.MemorySpace.SMEM)
     vmem = pl.BlockSpec(memory_space=VMEM)
+    table = lag_table()[: max(1, LAG_PASSES - 1)]
     return pl.pallas_call(
         lag_kernel,
         out_shape=jax.ShapeDtypeStruct((2, 4, SENSORS, LAGS), f32),
-        in_specs=[smem] + [vmem] * 6,
+        in_specs=[smem, smem] + [vmem] * 6,
         out_specs=vmem,
         scratch_shapes=[pltpu.VMEM((CANDS, 2, SENSORS, LAGS), f32)],
         compiler_params=pltpu.CompilerParams(vmem_limit_bytes=LIMIT),
-        cost_estimate=pl.CostEstimate(flops=2 * 10**8, bytes_accessed=3 * 10**6, transcendentals=0),
+        cost_estimate=pl.CostEstimate(flops=10**5, bytes_accessed=10**4, transcendentals=0),
         name="lag",
-    )(slots, jnp.asarray(lag_table()), mask, *got)
+    )(tile, blocks, mask, jnp.asarray(table), *got)
 
 
 def per_device(raw, blocks, mask):
     tiles = lax.axis_size("tile")
-    tile = lax.axis_index("tile")
-    core = tile % 2
-    relative = blocks - tile
-    other = 1 - 2 * core
-    slots = jnp.where(
-        relative == other,
-        0,
-        jnp.where(relative == -other, 3, jnp.where(relative == 2 * other, 1, 2)),
-    ).astype(jnp.int32)
+    tile = lax.axis_index("tile").astype(jnp.int32).reshape(1)
     turn = lax.axis_index("tm").astype(jnp.int32).reshape(1)
-    wide_mask = jnp.broadcast_to(mask.astype(f32)[..., None], mask.shape + (LANE,))
 
     def ring(block, distances):
         route = [(i, (i + distances[i % 2]) % tiles) for i in range(tiles)]
@@ -370,15 +379,16 @@
     near = ring(spectra, (1, -1))
     ahead = ring(spectra, (-2, 2))
     behind = ring(spectra, (2, -2))
-    corner = ring(ahead, (1, -1))
     own, mine = own_of(turn, spectra)
     s_cross, s_power = cross_of(own, near)
+    ahead, s_power = lax.optimization_barrier((ahead, s_power))
+    corner = ring(ahead, (1, -1))
     a_cross, a_power = cross_of(own, ahead)
     messages = messages_of(
         own, behind, corner, s_cross, s_power, a_cross, a_power, mine
     )
-    got = [messages[0]] + [onward(messages[k], k) for k in (2, 1, 3)]
-    return lag_of(slots, wide_mask, *got)
+    got = [messages[0]] + [onward(messages[k], k) for k in (3, 1, 2)]
+    return lag_of(tile, blocks, mask, *got)
 
 
 def solution(mesh):

time: 38.6 us -> 35.7 us (0.925)
  the two profiles are of different devices: /device:TPU:1 before, /device:TPU:0 now
where the time goes in v3:
time: 35.7 us; the launch traced here: 35.6 us
  waiting for transfers between devices  16 us (45%)
  starting transfers between devices  11.8 us (33%)
  Pallas kernels  7.77 us (22%)
    ppermute x4, waiting for transfers between devices, ring(): return lax.ppermute(block, 'tile', route)  8.08 us
    ppermute x3, waiting for transfers between devices, onward(): lax.ppermute(block, 'tm', [(i, (i + distance) % groups) for i in range(gr...  7.89 us
    ppermute x4, starting transfers between devices, ring(): return lax.ppermute(block, 'tile', route)  6.49 us
    ppermute x3, starting transfers between devices, onward(): lax.ppermute(block, 'tm', [(i, (i + distance) % groups) for i in range(gr...  5.3 us
    pallas_call x1, Pallas kernels, spectra_of(): pl.pallas_call(spectra_kernel, out_shape=pltpu.VMEM((ROWS, LENGTH), bf16)...  3.14 us
    pallas_call x1, Pallas kernels, lag_of(): pl.pallas_call(lag_kernel, out_shape=jax.ShapeDtypeStruct((2, 4, SENSORS,...  1.54 us
    pallas_call x1, Pallas kernels, messages_of(): pl.pallas_call(message_kernel, out_shape=(pltpu.VMEM((MESSAGE, LENGTH), b...  1.51 us
    pallas_call x2, Pallas kernels, cross_of(): pl.pallas_call(cross_kernel, out_shape=(pltpu.VMEM((4, PAIRS, LENGTH), bf...  1.49 us
  transfers between devices with their start and end apart: 7, of which 4 were waited for; matrix products, arithmetic and copies ran while one was open for 0% of the time, Pallas kernels for 4%

profile of v3, /device:TPU:0, one launch (start us, length us, event | category | flops | bytes accessed | tf_op | source)
XLA Modules:
  0.0 35.6 jit_solution(1830210113090336344)
XLA Ops:
  0.0 3.1 %spectra.1.spectra_ref = bf16[128,1024]{1,0:T(8,128)(2,1)S(1)} custom-call(bf16[16,8,4,1039]{3,2,1,0:T(4,128)(2,1)} %raw_hbm.1, bf16[4,256,256]{2,1,0:T(8,128)(2,1)} %constant.15.clone.fir_hbm, bf16[1024,1024]{1,0:T(8,128)(2,1)} %constant.16.clone.dft_hbm), custom_call_target="tpu_custom_call" | custom-call | flops 100000 | bytes 10000 | tf_op jit(solution)/shard_map/spectra/pallas_call | solution.py:139
  3.2 0.0 copy-start
  3.2 0.0 copy-start.1
  3.2 0.0 copy-start.2
  3.2 0.1 collective-permute-start.2
  3.3 6.4 %collective-permute-start.1 = (bf16[128,1024]{1,0:T(8,128)(2,1)S(1)}, bf16[128,1024]{1,0:T(8,128)(2,1)S(1)}, u32[]{:S(2)}, u32[]{:S(2)}) collective-permute-start(bf16[128,1024]{1,0:T(8,128)(2,1)S(1)} %spectra.1.spectra_ref), channel_id=1, source_target_pairs={{0,248},{4,12},{8,0},{12,20},{16,8},{20,28},{24,16},{28,36},{32,24... | collective-permute-start | bytes 786440 | tf_op jit(solution)/shard_map/ppermute | solution.py:372
  9.7 0.0 collective-permute-start
  9.7 0.1 own.1
  9.8 0.0 collective-permute-done.2.far_ref
  9.8 0.7 %cross.2 = (bf16[4,16,1024]{2,1,0:T(8,128)(2,1)S(1)}, f32[8,512]{1,0:T(8,128)S(1)}) custom-call(f32[128,1024]{1,0:T(8,128)S(1)} %get-tuple-element.17.own_ref, bf16[128,1024]{1,0:T(8,128)(2,1)S(1)} %collective-permute-done.2.far_ref), custom_call_target="tpu_custom_call" | custom-call | flops 100000 | bytes 10000 | tf_op jit(solution)/shard_map/cross/pallas_call | solution.py:208
  10.5 5.3 %collective-permute-done.1.far_ref = bf16[128,1024]{1,0:T(8,128)(2,1)S(1)} collective-permute-done((bf16[128,1024]{1,0:T(8,128)(2,1)S(1)}, bf16[128,1024]{1,0:T(8,128)(2,1)S(1)}, u32[]{:S(2)}, u32[]{:S(2)}) %collective-permute-start.1) | collective-permute-done | bytes 262176 | tf_op jit(solution)/shard_map/ppermute | solution.py:372
  15.8 0.0 collective-permute-start.3
  15.9 0.7 %cross.3 = (bf16[4,16,1024]{2,1,0:T(8,128)(2,1)S(1)}, f32[8,512]{1,0:T(8,128)S(1)}) custom-call(f32[128,1024]{1,0:T(8,128)S(1)} %get-tuple-element.17.own_ref, bf16[128,1024]{1,0:T(8,128)(2,1)S(1)} %collective-permute-done.1.far_ref), custom_call_target="tpu_custom_call" | custom-call | flops 100000 | bytes 10000 | tf_op jit(solution)/shard_map/cross/pallas_call | solution.py:208
  16.6 2.8 %collective-permute-done.third_ref = bf16[128,1024]{1,0:T(8,128)(2,1)S(1)} collective-permute-done((bf16[128,1024]{1,0:T(8,128)(2,1)S(1)}, bf16[128,1024]{1,0:T(8,128)(2,1)S(1)}, u32[]{:S(2)}, u32[]{:S(2)}) %collective-permute-start) | collective-permute-done | bytes 262176 | tf_op jit(solution)/shard_map/ppermute | solution.py:372
  19.4 0.0 collective-permute-done.3.fourth_ref
  19.4 1.5 %message.1 = (bf16[96,1024]{1,0:T(8,128)(2,1)S(1)}, bf16[96,1024]{1,0:T(8,128)(2,1)S(1)}, bf16[96,1024]{1,0:T(8,128)(2,1)S(1)}, bf16[96,1024]{1,0:T(8,128)(2,1)S(1)}) custom-call(f32[128,1024]{1,0:T(8,128)S(1)} %get-tuple-element.17.own_ref, bf16[128,1024]{1,0:T(8,128)(2,1)S(1)} %collective-permute-done.third_ref, ...), custom_call_target="tpu_custom_call" | custom-call | flops 100000 | bytes 10000 | tf_op jit(solution)/shard_map/message/pallas_call | solution.py:283
  20.9 3.1 %collective-permute-start.4 = (bf16[96,1024]{1,0:T(8,128)(2,1)S(1)}, bf16[96,1024]{1,0:T(8,128)(2,1)S(1)}, u32[]{:S(2)}, u32[]{:S(2)}) collective-permute-start(bf16[96,1024]{1,0:T(8,128)(2,1)S(1)} %get-tuple-element.26), channel_id=1, source_target_pairs={{0,3},{1,0},{2,1},{3,2},{4,7},{5,4},{6,5},{7,6},{8,11},{9,8},{10,9... | collective-permute-start | bytes 589832 | tf_op jit(solution)/shard_map/ppermute | solution.py:376
  24.0 0.0 collective-permute-start.5
  24.0 2.2 %collective-permute-start.6 = (bf16[96,1024]{1,0:T(8,128)(2,1)S(1)}, bf16[96,1024]{1,0:T(8,128)(2,1)S(1)}, u32[]{:S(2)}, u32[]{:S(2)}) collective-permute-start(bf16[96,1024]{1,0:T(8,128)(2,1)S(1)} %get-tuple-element.28), channel_id=1, source_target_pairs={{0,2},{1,3},{2,0},{3,1},{4,6},{5,7},{6,4},{7,5},{8,10},{9,11},{10,... | collective-permute-start | bytes 589832 | tf_op jit(solution)/shard_map/ppermute | solution.py:376
  26.2 5.2 %collective-permute-done.4.refs_1_ = bf16[96,1024]{1,0:T(8,128)(2,1)S(1)} collective-permute-done((bf16[96,1024]{1,0:T(8,128)(2,1)S(1)}, bf16[96,1024]{1,0:T(8,128)(2,1)S(1)}, u32[]{:S(2)}, u32[]{:S(2)}) %collective-permute-start.4) | collective-permute-done | bytes 196640 | tf_op jit(solution)/shard_map/ppermute | solution.py:376
  31.4 2.7 %collective-permute-done.5.refs_2_ = bf16[96,1024]{1,0:T(8,128)(2,1)S(1)} collective-permute-done((bf16[96,1024]{1,0:T(8,128)(2,1)S(1)}, bf16[96,1024]{1,0:T(8,128)(2,1)S(1)}, u32[]{:S(2)}, u32[]{:S(2)}) %collective-permute-start.5) | collective-permute-done | bytes 196640 | tf_op jit(solution)/shard_map/ppermute | solution.py:376
  34.1 0.0 collective-permute-done.6.refs_3_
  34.1 0.0 copy-done
  34.1 1.5 %lag.1 = f32[2,4,8,512]{3,2,1,0:T(8,128)} custom-call(s32[1]{0:T(128)} %bitcast.tile_ref, s32[4]{0:T(128)S(1)} %copy-done.2, s32[2,4,8]{2,1,0:T(4,128)S(1)} %copy-done.1, bf16[1,1024,512]{2,1,0:T(8,128)(2,1)S(1)} %copy-done, bf16[96,1024]{1,0:T(8,128)(2,1)S(1)} %get-tuple-element.25.refs_0_, bf16[96,1024]{1,0:T(8,128)(2,1)S(1)} %collective-permute-done.4.refs_1_, ...), custom_call_target="tpu_custom_call" | custom-call | flops 100000 | bytes 10000 | tf_op jit(solution)/shard_map/lag/pallas_call | solution.py:353
  (2 shorter events, 0.0 us)
Async XLA Ops:
  3.2 30.9 %copy-start = (bf16[1,1024,512]{2,1,0:T(8,128)(2,1)S(1)}, bf16[1,1024,512]{2,1,0:T(8,128)(2,1)}, u32[]{:S(2)}) copy-start(bf16[1,1024,512]{2,1,0:T(8,128)(2,1)} %constant.17.clone.table_ref) | copy-start | bytes 3145732
  3.2 30.9 %copy-start.1 = (s32[2,4,8]{2,1,0:T(4,128)S(1)}, s32[2,4,8]{2,1,0:T(4,128)}, u32[]{:S(2)}) copy-start(s32[2,4,8]{2,1,0:T(4,128)} %mask_ref.1) | copy-start | bytes 772
  3.2 30.9 %copy-start.2 = (s32[4]{0:T(128)S(1)}, s32[4]{0:T(128)}, u32[]{:S(2)}) copy-start(s32[4]{0:T(128)} %blocks_ref.1) | copy-start | bytes 52
  3.2 6.6 %collective-permute-start.2 = (bf16[128,1024]{1,0:T(8,128)(2,1)S(1)}, bf16[128,1024]{1,0:T(8,128)(2,1)S(1)}, u32[]{:S(2)}, u32[]{:S(2)}) collective-permute-start(bf16[128,1024]{1,0:T(8,128)(2,1)S(1)} %spectra.1.spectra_ref), channel_id=1, source_target_pairs={{0,4},{4,0},{8,12},{12,8},{16,20},{20,16},{24,28},{28,24},{32,36},... | collective-permute-start | bytes 786440 | tf_op jit(solution)/shard_map/ppermute | solution.py:372
  3.3 12.6 %collective-permute-start.1 = (bf16[128,1024]{1,0:T(8,128)(2,1)S(1)}, bf16[128,1024]{1,0:T(8,128)(2,1)S(1)}, u32[]{:S(2)}, u32[]{:S(2)}) collective-permute-start(bf16[128,1024]{1,0:T(8,128)(2,1)S(1)} %spectra.1.spectra_ref), channel_id=1, source_target_pairs={{0,248},{4,12},{8,0},{12,20},{16,8},{20,28},{24,16},{28,36},{32,24... | collective-permute-start | bytes 786440 | tf_op jit(solution)/shard_map/ppermute | solution.py:372
  9.7 9.7 %collective-permute-start = (bf16[128,1024]{1,0:T(8,128)(2,1)S(1)}, bf16[128,1024]{1,0:T(8,128)(2,1)S(1)}, u32[]{:S(2)}, u32[]{:S(2)}) collective-permute-start(bf16[128,1024]{1,0:T(8,128)(2,1)S(1)} %spectra.1.spectra_ref), channel_id=1, source_target_pairs={{0,8},{4,252},{8,16},{12,4},{16,24},{20,12},{24,32},{28,20},{32,40... | collective-permute-start | bytes 786440 | tf_op jit(solution)/shard_map/ppermute | solution.py:372
  15.8 3.5 %collective-permute-start.3 = (bf16[128,1024]{1,0:T(8,128)(2,1)S(1)}, bf16[128,1024]{1,0:T(8,128)(2,1)S(1)}, u32[]{:S(2)}, u32[]{:S(2)}) collective-permute-start(bf16[128,1024]{1,0:T(8,128)(2,1)S(1)} %collective-permute-done.1.far_ref), channel_id=1, source_target_pairs={{0,4},{4,0},{8,12},{12,8},{16,20},{20,16},{24,28},{28,24},{32,36},... | collective-permute-start | bytes 786440 | tf_op jit(solution)/shard_map/ppermute | solution.py:372
  20.9 10.5 %collective-permute-start.4 = (bf16[96,1024]{1,0:T(8,128)(2,1)S(1)}, bf16[96,1024]{1,0:T(8,128)(2,1)S(1)}, u32[]{:S(2)}, u32[]{:S(2)}) collective-permute-start(bf16[96,1024]{1,0:T(8,128)(2,1)S(1)} %get-tuple-element.26), channel_id=1, source_target_pairs={{0,3},{1,0},{2,1},{3,2},{4,7},{5,4},{6,5},{7,6},{8,11},{9,8},{10,9... | collective-permute-start | bytes 589832 | tf_op jit(solution)/shard_map/ppermute | solution.py:376
  24.0 10.1 %collective-permute-start.5 = (bf16[96,1024]{1,0:T(8,128)(2,1)S(1)}, bf16[96,1024]{1,0:T(8,128)(2,1)S(1)}, u32[]{:S(2)}, u32[]{:S(2)}) collective-permute-start(bf16[96,1024]{1,0:T(8,128)(2,1)S(1)} %get-tuple-element.27), channel_id=1, source_target_pairs={{0,1},{1,2},{2,3},{3,0},{4,5},{5,6},{6,7},{7,4},{8,9},{9,10},{10,1... | collective-permute-start | bytes 589832 | tf_op jit(solution)/shard_map/ppermute | solution.py:376
  24.0 10.1 %collective-permute-start.6 = (bf16[96,1024]{1,0:T(8,128)(2,1)S(1)}, bf16[96,1024]{1,0:T(8,128)(2,1)S(1)}, u32[]{:S(2)}, u32[]{:S(2)}) collective-permute-start(bf16[96,1024]{1,0:T(8,128)(2,1)S(1)} %get-tuple-element.28), channel_id=1, source_target_pairs={{0,2},{1,3},{2,0},{3,1},{4,6},{5,7},{6,4},{7,5},{8,10},{9,11},{10,... | collective-permute-start | bytes 589832 | tf_op jit(solution)/shard_map/ppermute | solution.py:376

commit v4 on v3

--- a/solution.py
+++ b/solution.py
@@ -23,7 +23,7 @@
 SCALE = 2.0**32
 PAIRS = 2 * SENSORS
 CANDS = 4
-MESSAGE = CANDS * PAIRS + 32
+MESSAGE = CANDS * PAIRS + 16 + SENSORS
 VMEM = pltpu.MemorySpace.VMEM
 CHUNKS = 4
 LAG_PASSES = 2
@@ -220,18 +220,25 @@
 
 
 def own_kernel(turn_ref, spectra_ref, own_ref, mine_ref):
-    shift = lax.rem(SENSORS - 2 * turn_ref[0], SENSORS)
+    turn = turn_ref[0]
     power = jnp.zeros((SENSORS, BINS), f32)
+    sensor = lax.broadcasted_iota(jnp.int32, (SENSORS, LENGTH), 0)
+    upper = lax.rem(sensor, 4) >= 2
+    odd = lax.rem(turn, 2) == 1
+    high = turn >= 2
     for window in range(WIN):
         rows = slice(SENSORS * window, SENSORS * (window + 1))
-        block = pltpu.roll(spectra_ref[rows].astype(f32), shift, 0)
+        block = spectra_ref[rows].astype(f32)
+        swapped = jnp.where(upper, pltpu.roll(block, 2, 0), pltpu.roll(block, SENSORS - 2, 0))
+        block = jnp.where(odd, swapped, block)
+        block = jnp.where(high, pltpu.roll(block, 4, 0), block)
         own_ref[rows] = block
         square = block * block
         power = power + (square[:, :BINS] + square[:, BINS:])
-    high = power.astype(bf16).astype(f32)
-    mine = jnp.concatenate([high, power - high], axis=1)
+    rounded = power.astype(bf16).astype(f32)
+    mine = jnp.concatenate([rounded, power - rounded], axis=1)
     for k in range(4):
-        mine_ref[k] = jnp.concatenate([mine[2 * k : 2 * k + 2]] * SENSORS, axis=0).astype(bf16)
+        mine_ref[k] = jnp.concatenate([mine[2 * k : 2 * k + 2]] * 4, axis=0)
 
 
 def own_of(turn, spectra):
@@ -240,7 +247,7 @@
         own_kernel,
         out_shape=(
             pltpu.VMEM((ROWS, LENGTH), f32),
-            pltpu.VMEM((4, 16, LENGTH), bf16),
+            pltpu.VMEM((4, SENSORS, LENGTH), f32),
         ),
         in_specs=[pl.BlockSpec(memory_space=pltpu.MemorySpace.SMEM), vmem],
         out_specs=(vmem, vmem),
@@ -251,22 +258,19 @@
 
 
 def message_kernel(
-    own_ref, third_ref, fourth_ref, s_ref, sp_ref, a_ref, ap_ref, mine_ref, *out_refs
+    own_ref, far_ref, s_ref, sp_ref, a_ref, ap_ref, b_ref, bp_ref, mine_ref, *out_refs
 ):
-    powers = {0: sp_ref[...], 1: ap_ref[...]}
-    for slot, far_ref in ((2, third_ref), (3, fourth_ref)):
-        collected = []
-
-        def store(real, imag, first, second, third, power):
-            put_cross(out_refs, slot * PAIRS, real, imag, first, second, third)
-            collected.append(power)
-
-        cross_body(own_ref, far_ref, store)
-        powers[slot] = jnp.concatenate(collected, axis=1)
+    collected = []
+
+    def store(real, imag, first, second, third, power):
+        put_cross(out_refs, 3 * PAIRS, real, imag, first, second, third)
+        collected.append(power)
+
+    cross_body(own_ref, far_ref, store)
     near = jnp.concatenate(
         [
-            jnp.concatenate([powers[0], powers[1]], axis=1),
-            jnp.concatenate([powers[2], powers[3]], axis=1),
+            jnp.concatenate([sp_ref[...], ap_ref[...]], axis=1),
+            jnp.concatenate([bp_ref[...], jnp.concatenate(collected, axis=1)], axis=1),
         ],
         axis=0,
     ).astype(bf16)
@@ -274,8 +278,9 @@
     for k in range(4):
         out_refs[k][0:PAIRS] = s_ref[k]
         out_refs[k][PAIRS : 2 * PAIRS] = a_ref[k]
+        out_refs[k][2 * PAIRS : 3 * PAIRS] = b_ref[k]
         out_refs[k][base : base + 16] = near
-        out_refs[k][base + 16 : base + 32] = mine_ref[k]
+        out_refs[k][base + 16 : MESSAGE] = mine_ref[k].astype(bf16)
 
 
 def messages_of(*parts):
@@ -283,7 +288,7 @@
     return pl.pallas_call(
         message_kernel,
         out_shape=(pltpu.VMEM((MESSAGE, LENGTH), bf16),) * 4,
-        in_specs=[vmem] * 8,
+        in_specs=[vmem] * len(parts),
         out_specs=(vmem,) * 4,
         compiler_params=pltpu.CompilerParams(vmem_limit_bytes=LIMIT),
         cost_estimate=pl.CostEstimate(flops=10**5, bytes_accessed=10**4, transcendentals=0),
@@ -303,7 +308,7 @@
         return lax.rsqrt(power / (4 * WIN) + 1e-06 * SCALE * SCALE)
 
     near = inverse(summed(slice(base, base + 16)))
-    mine = summed(slice(base + 16, base + 32))
+    mine = summed(slice(base + 16, MESSAGE))
     mine = inverse(mine[:, :BINS] + mine[:, BINS:])
     own = [mine[i : i + 1] for i in range(2)]
     pieces = []
@@ -368,12 +373,14 @@
     turn = lax.axis_index("tm").astype(jnp.int32).reshape(1)
 
     def ring(block, distances):
-        route = [(i, (i + distances[i % 2]) % tiles) for i in range(tiles)]
-        return lax.ppermute(block, "tile", route)
-
-    def onward(block, distance):
-        groups = lax.axis_size("tm")
-        return lax.ppermute(block, "tm", [(i, (i + distance) % groups) for i in range(groups)])
+        def target(i):
+            there = i + distances[i % 2]
+            return there if 0 <= there < tiles else i + 1 - 2 * (i % 2)
+
+        return lax.ppermute(block, "tile", [(i, target(i)) for i in range(tiles)])
+
+    def onward(block, step):
+        return lax.ppermute(block, "tm", [(i, i ^ step) for i in range(lax.axis_size("tm"))])
 
     spectra = spectra_of(raw)
     near = ring(spectra, (1, -1))
@@ -384,10 +391,11 @@
     ahead, s_power = lax.optimization_barrier((ahead, s_power))
     corner = ring(ahead, (1, -1))
     a_cross, a_power = cross_of(own, ahead)
+    b_cross, b_power = cross_of(own, behind)
     messages = messages_of(
-        own, behind, corner, s_cross, s_power, a_cross, a_power, mine
+        own, corner, s_cross, s_power, a_cross, a_power, b_cross, b_power, mine
     )
-    got = [messages[0]] + [onward(messages[k], k) for k in (3, 1, 2)]
+    got = [messages[0]] + [onward(messages[k], k) for k in (3, 2, 1)]
     return lag_of(tile, blocks, mask, *got)
 
 

time: 35.7 us -> 31.4 us (0.88)
  the two profiles are of different devices: /device:TPU:0 before, /device:TPU:198 now
where the time goes in v4:
time: 31.4 us; the launch traced here: 31.3 us
  waiting for transfers between devices  14.8 us (47%)
  starting transfers between devices  8.51 us (27%)
  Pallas kernels  7.87 us (25%)
    ppermute x3, waiting for transfers between devices, onward(): lax.ppermute(block, 'tm', [(i, i ^ step) for i in range(lax.axis_size('tm...  8.7 us
    ppermute x4, waiting for transfers between devices, ring(): return lax.ppermute(block, 'tile', [(i, target(i)) for i in range(tiles)])  6.14 us
    ppermute x4, starting transfers between devices, ring(): return lax.ppermute(block, 'tile', [(i, target(i)) for i in range(tiles)])  4.31 us
    ppermute x3, starting transfers between devices, onward(): lax.ppermute(block, 'tm', [(i, i ^ step) for i in range(lax.axis_size('tm...  4.2 us
    pallas_call x1, Pallas kernels, spectra_of(): pl.pallas_call(spectra_kernel, out_shape=pltpu.VMEM((ROWS, LENGTH), bf16)...  3.14 us
    pallas_call x3, Pallas kernels, cross_of(): pl.pallas_call(cross_kernel, out_shape=(pltpu.VMEM((4, PAIRS, LENGTH), bf...  2.23 us
    pallas_call x1, Pallas kernels, lag_of(): pl.pallas_call(lag_kernel, out_shape=jax.ShapeDtypeStruct((2, 4, SENSORS,...  1.54 us
    pallas_call x1, Pallas kernels, messages_of(): pl.pallas_call(message_kernel, out_shape=(pltpu.VMEM((MESSAGE, LENGTH), b...  0.78 us
  transfers between devices with their start and end apart: 7, of which 3 were waited for; matrix products, arithmetic and copies ran while one was open for 0% of the time, Pallas kernels for 8%

profile of v4, /device:TPU:198, one launch (start us, length us, event | category | flops | bytes accessed | tf_op | source)
XLA Modules:
  0.0 31.3 jit_solution(14222648781725356612)
XLA Ops:
  0.0 3.1 %spectra.1.spectra_ref = bf16[128,1024]{1,0:T(8,128)(2,1)S(1)} custom-call(bf16[16,8,4,1039]{3,2,1,0:T(4,128)(2,1)} %raw_hbm.1, bf16[4,256,256]{2,1,0:T(8,128)(2,1)} %constant.15.clone.fir_hbm, bf16[1024,1024]{1,0:T(8,128)(2,1)} %constant.16.clone.dft_hbm), custom_call_target="tpu_custom_call" | custom-call | flops 100000 | bytes 10000 | tf_op jit(solution)/shard_map/spectra/pallas_call | solution.py:139
  3.2 0.0 copy-start
  3.2 0.0 copy-start.1
  3.2 0.0 copy-start.2
  3.2 0.1 collective-permute-start.1
  3.3 0.9 %collective-permute-start = (bf16[128,1024]{1,0:T(8,128)(2,1)S(1)}, bf16[128,1024]{1,0:T(8,128)(2,1)S(1)}, u32[]{:S(2)}, u32[]{:S(2)}) collective-permute-start(bf16[128,1024]{1,0:T(8,128)(2,1)S(1)} %spectra.1.spectra_ref), channel_id=1, source_target_pairs={{0,4},{4,12},{8,0},{12,20},{16,8},{20,28},{24,16},{28,36},{32,24},... | collective-permute-start | bytes 786440 | tf_op jit(solution)/shard_map/ppermute | solution.py:380
  4.2 3.3 %collective-permute-start.3 = (bf16[128,1024]{1,0:T(8,128)(2,1)S(1)}, bf16[128,1024]{1,0:T(8,128)(2,1)S(1)}, u32[]{:S(2)}, u32[]{:S(2)}) collective-permute-start(bf16[128,1024]{1,0:T(8,128)(2,1)S(1)} %spectra.1.spectra_ref), channel_id=1, source_target_pairs={{0,8},{4,0},{8,16},{12,4},{16,24},{20,12},{24,32},{28,20},{32,40},... | collective-permute-start | bytes 786440 | tf_op jit(solution)/shard_map/ppermute | solution.py:380
  7.5 0.2 own.1
  7.7 0.0 collective-permute-done.1.far_ref
  7.7 0.7 %cross.3 = (bf16[4,16,1024]{2,1,0:T(8,128)(2,1)S(1)}, f32[8,512]{1,0:T(8,128)S(1)}) custom-call(f32[128,1024]{1,0:T(8,128)S(1)} %get-tuple-element.19.own_ref, bf16[128,1024]{1,0:T(8,128)(2,1)S(1)} %collective-permute-done.1.far_ref), custom_call_target="tpu_custom_call" | custom-call | flops 100000 | bytes 10000 | tf_op jit(solution)/shard_map/cross/pallas_call | solution.py:208
  8.4 6.1 %collective-permute-done.far_ref = bf16[128,1024]{1,0:T(8,128)(2,1)S(1)} collective-permute-done((bf16[128,1024]{1,0:T(8,128)(2,1)S(1)}, bf16[128,1024]{1,0:T(8,128)(2,1)S(1)}, u32[]{:S(2)}, u32[]{:S(2)}) %collective-permute-start) | collective-permute-done | bytes 262176 | tf_op jit(solution)/shard_map/ppermute | solution.py:380
  14.5 0.0 collective-permute-start.2
  14.6 0.7 %cross.4 = (bf16[4,16,1024]{2,1,0:T(8,128)(2,1)S(1)}, f32[8,512]{1,0:T(8,128)S(1)}) custom-call(f32[128,1024]{1,0:T(8,128)S(1)} %get-tuple-element.19.own_ref, bf16[128,1024]{1,0:T(8,128)(2,1)S(1)} %collective-permute-done.far_ref), custom_call_target="tpu_custom_call" | custom-call | flops 100000 | bytes 10000 | tf_op jit(solution)/shard_map/cross/pallas_call | solution.py:208
  15.3 0.0 collective-permute-done.3.far_ref
  15.3 0.7 %cross.5 = (bf16[4,16,1024]{2,1,0:T(8,128)(2,1)S(1)}, f32[8,512]{1,0:T(8,128)S(1)}) custom-call(f32[128,1024]{1,0:T(8,128)S(1)} %get-tuple-element.19.own_ref, bf16[128,1024]{1,0:T(8,128)(2,1)S(1)} %collective-permute-done.3.far_ref), custom_call_target="tpu_custom_call" | custom-call | flops 100000 | bytes 10000 | tf_op jit(solution)/shard_map/cross/pallas_call | solution.py:208
  16.1 0.0 collective-permute-done.2.far_ref
  16.1 0.8 %message.1 = (bf16[88,1024]{1,0:T(8,128)(2,1)S(1)}, bf16[88,1024]{1,0:T(8,128)(2,1)S(1)}, bf16[88,1024]{1,0:T(8,128)(2,1)S(1)}, bf16[88,1024]{1,0:T(8,128)(2,1)S(1)}) custom-call(f32[128,1024]{1,0:T(8,128)S(1)} %get-tuple-element.19.own_ref, bf16[128,1024]{1,0:T(8,128)(2,1)S(1)} %collective-permute-done.2.far_ref, ...), custom_call_target="tpu_custom_call" | custom-call | flops 100000 | bytes 10000 | tf_op jit(solution)/shard_map/message/pallas_call | solution.py:288
  16.9 3.1 %collective-permute-start.4 = (bf16[88,1024]{1,0:T(8,128)(2,1)S(1)}, bf16[88,1024]{1,0:T(8,128)(2,1)S(1)}, u32[]{:S(2)}, u32[]{:S(2)}) collective-permute-start(bf16[88,1024]{1,0:T(8,128)(2,1)S(1)} %get-tuple-element.30), channel_id=1, source_target_pairs={{0,3},{1,2},{2,1},{3,0},{4,7},{5,6},{6,5},{7,4},{8,11},{9,10},{10,... | collective-permute-start | bytes 540680 | tf_op jit(solution)/shard_map/ppermute | solution.py:383
  20.0 0.6 %collective-permute-start.5 = (bf16[88,1024]{1,0:T(8,128)(2,1)S(1)}, bf16[88,1024]{1,0:T(8,128)(2,1)S(1)}, u32[]{:S(2)}, u32[]{:S(2)}) collective-permute-start(bf16[88,1024]{1,0:T(8,128)(2,1)S(1)} %get-tuple-element.31), channel_id=1, source_target_pairs={{0,2},{1,3},{2,0},{3,1},{4,6},{5,7},{6,4},{7,5},{8,10},{9,11},{10,... | collective-permute-start | bytes 540680 | tf_op jit(solution)/shard_map/ppermute | solution.py:383
  20.6 0.5 %collective-permute-start.6 = (bf16[88,1024]{1,0:T(8,128)(2,1)S(1)}, bf16[88,1024]{1,0:T(8,128)(2,1)S(1)}, u32[]{:S(2)}, u32[]{:S(2)}) collective-permute-start(bf16[88,1024]{1,0:T(8,128)(2,1)S(1)} %get-tuple-element.32), channel_id=1, source_target_pairs={{0,1},{1,0},{2,3},{3,2},{4,5},{5,4},{6,7},{7,6},{8,9},{9,8},{10,11... | collective-permute-start | bytes 540680 | tf_op jit(solution)/shard_map/ppermute | solution.py:383
  21.1 8.0 %collective-permute-done.4.refs_1_ = bf16[88,1024]{1,0:T(8,128)(2,1)S(1)} collective-permute-done((bf16[88,1024]{1,0:T(8,128)(2,1)S(1)}, bf16[88,1024]{1,0:T(8,128)(2,1)S(1)}, u32[]{:S(2)}, u32[]{:S(2)}) %collective-permute-start.4) | collective-permute-done | bytes 180256 | tf_op jit(solution)/shard_map/ppermute | solution.py:383
  29.0 0.0 collective-permute-done.5.refs_2_
  29.0 0.7 %collective-permute-done.6.refs_3_ = bf16[88,1024]{1,0:T(8,128)(2,1)S(1)} collective-permute-done((bf16[88,1024]{1,0:T(8,128)(2,1)S(1)}, bf16[88,1024]{1,0:T(8,128)(2,1)S(1)}, u32[]{:S(2)}, u32[]{:S(2)}) %collective-permute-start.6) | collective-permute-done | bytes 180256 | tf_op jit(solution)/shard_map/ppermute | solution.py:383
  29.8 1.5 %lag.1 = f32[2,4,8,512]{3,2,1,0:T(8,128)} custom-call(s32[1]{0:T(128)} %bitcast.tile_ref, s32[4]{0:T(128)S(1)} %copy-done.2, s32[2,4,8]{2,1,0:T(4,128)S(1)} %copy-done.1, bf16[1,1024,512]{2,1,0:T(8,128)(2,1)S(1)} %copy-done, bf16[88,1024]{1,0:T(8,128)(2,1)S(1)} %get-tuple-element.29.refs_0_, bf16[88,1024]{1,0:T(8,128)(2,1)S(1)} %collective-permute-done.4.refs_1_, ...), custom_call_target="tpu_custom_call" | custom-call | flops 100000 | bytes 10000 | tf_op jit(solution)/shard_map/lag/pallas_call | solution.py:358
  (3 shorter events, 0.0 us)
Async XLA Ops:
  3.2 26.6 %copy-start = (bf16[1,1024,512]{2,1,0:T(8,128)(2,1)S(1)}, bf16[1,1024,512]{2,1,0:T(8,128)(2,1)}, u32[]{:S(2)}) copy-start(bf16[1,1024,512]{2,1,0:T(8,128)(2,1)} %constant.17.clone.table_ref) | copy-start | bytes 3145732
  3.2 26.6 %copy-start.1 = (s32[2,4,8]{2,1,0:T(4,128)S(1)}, s32[2,4,8]{2,1,0:T(4,128)}, u32[]{:S(2)}) copy-start(s32[2,4,8]{2,1,0:T(4,128)} %mask_ref.1) | copy-start | bytes 772
  3.2 26.6 %copy-start.2 = (s32[4]{0:T(128)S(1)}, s32[4]{0:T(128)}, u32[]{:S(2)}) copy-start(s32[4]{0:T(128)} %blocks_ref.1) | copy-start | bytes 52
  3.2 4.5 %collective-permute-start.1 = (bf16[128,1024]{1,0:T(8,128)(2,1)S(1)}, bf16[128,1024]{1,0:T(8,128)(2,1)S(1)}, u32[]{:S(2)}, u32[]{:S(2)}) collective-permute-start(bf16[128,1024]{1,0:T(8,128)(2,1)S(1)} %spectra.1.spectra_ref), channel_id=1, source_target_pairs={{0,4},{4,0},{8,12},{12,8},{16,20},{20,16},{24,28},{28,24},{32,36},... | collective-permute-start | bytes 786440 | tf_op jit(solution)/shard_map/ppermute | solution.py:380
  3.3 11.3 %collective-permute-start = (bf16[128,1024]{1,0:T(8,128)(2,1)S(1)}, bf16[128,1024]{1,0:T(8,128)(2,1)S(1)}, u32[]{:S(2)}, u32[]{:S(2)}) collective-permute-start(bf16[128,1024]{1,0:T(8,128)(2,1)S(1)} %spectra.1.spectra_ref), channel_id=1, source_target_pairs={{0,4},{4,12},{8,0},{12,20},{16,8},{20,28},{24,16},{28,36},{32,24},... | collective-permute-start | bytes 786440 | tf_op jit(solution)/shard_map/ppermute | solution.py:380
  4.2 11.1 %collective-permute-start.3 = (bf16[128,1024]{1,0:T(8,128)(2,1)S(1)}, bf16[128,1024]{1,0:T(8,128)(2,1)S(1)}, u32[]{:S(2)}, u32[]{:S(2)}) collective-permute-start(bf16[128,1024]{1,0:T(8,128)(2,1)S(1)} %spectra.1.spectra_ref), channel_id=1, source_target_pairs={{0,8},{4,0},{8,16},{12,4},{16,24},{20,12},{24,32},{28,20},{32,40},... | collective-permute-start | bytes 786440 | tf_op jit(solution)/shard_map/ppermute | solution.py:380
  14.5 1.5 %collective-permute-start.2 = (bf16[128,1024]{1,0:T(8,128)(2,1)S(1)}, bf16[128,1024]{1,0:T(8,128)(2,1)S(1)}, u32[]{:S(2)}, u32[]{:S(2)}) collective-permute-start(bf16[128,1024]{1,0:T(8,128)(2,1)S(1)} %collective-permute-done.far_ref), channel_id=1, source_target_pairs={{0,4},{4,0},{8,12},{12,8},{16,20},{20,16},{24,28},{28,24},{32,36},... | collective-permute-start | bytes 786440 | tf_op jit(solution)/shard_map/ppermute | solution.py:380
  16.9 12.2 %collective-permute-start.4 = (bf16[88,1024]{1,0:T(8,128)(2,1)S(1)}, bf16[88,1024]{1,0:T(8,128)(2,1)S(1)}, u32[]{:S(2)}, u32[]{:S(2)}) collective-permute-start(bf16[88,1024]{1,0:T(8,128)(2,1)S(1)} %get-tuple-element.30), channel_id=1, source_target_pairs={{0,3},{1,2},{2,1},{3,0},{4,7},{5,6},{6,5},{7,4},{8,11},{9,10},{10,... | collective-permute-start | bytes 540680 | tf_op jit(solution)/shard_map/ppermute | solution.py:383
  20.0 9.1 %collective-permute-start.5 = (bf16[88,1024]{1,0:T(8,128)(2,1)S(1)}, bf16[88,1024]{1,0:T(8,128)(2,1)S(1)}, u32[]{:S(2)}, u32[]{:S(2)}) collective-permute-start(bf16[88,1024]{1,0:T(8,128)(2,1)S(1)} %get-tuple-element.31), channel_id=1, source_target_pairs={{0,2},{1,3},{2,0},{3,1},{4,6},{5,7},{6,4},{7,5},{8,10},{9,11},{10,... | collective-permute-start | bytes 540680 | tf_op jit(solution)/shard_map/ppermute | solution.py:383
  20.6 9.2 %collective-permute-start.6 = (bf16[88,1024]{1,0:T(8,128)(2,1)S(1)}, bf16[88,1024]{1,0:T(8,128)(2,1)S(1)}, u32[]{:S(2)}, u32[]{:S(2)}) collective-permute-start(bf16[88,1024]{1,0:T(8,128)(2,1)S(1)} %get-tuple-element.32), channel_id=1, source_target_pairs={{0,1},{1,0},{2,3},{3,2},{4,5},{5,4},{6,7},{7,6},{8,9},{9,8},{10,11... | collective-permute-start | bytes 540680 | tf_op jit(solution)/shard_map/ppermute | solution.py:383

commit v5 on v4

--- a/solution.py
+++ b/solution.py
@@ -15,11 +15,13 @@
 DEC = 4
 REACH = 2
 BINS = 512
+HALF = BINS // 2
 LENGTH = 2 * BINS
 SENSORS = 8
 WIN = 16
 ROWS = WIN * SENSORS
 LANE = 128
+REACHED = LANE + 16
 SCALE = 2.0**32
 PAIRS = 2 * SENSORS
 CANDS = 4
@@ -44,29 +46,39 @@
     taper = 0.5 - 0.5 * np.cos(2.0 * np.pi * (index + 0.5) / TAPS)
     taps = (np.sinc(centred) * taper / DEC).astype(np.float32)
     high, low = split_high_low(taps)
-    table = np.zeros((DEC, 2 * LANE, 2 * LANE), ml_dtypes.bfloat16)
-    column = np.arange(LANE)
+    table = np.zeros((DEC, REACHED, 2 * LANE), ml_dtypes.bfloat16)
+    sample = np.arange(LANE)
+    column = sample // 2 + (sample % 2) * (LANE // 2)
     for phase in range(DEC):
         for offset in range(TAPS // DEC):
-            table[phase, column + offset, column] = high[DEC * offset + phase]
-            table[phase, column + offset, LANE + column] = low[DEC * offset + phase]
+            table[phase, sample + offset, column] = high[DEC * offset + phase]
+            table[phase, sample + offset, LANE + column] = low[DEC * offset + phase]
     return table
 
 
+def angles(left, right):
+    return np.mod(left * right, LENGTH).astype(np.float64) * (2.0 * np.pi / LENGTH)
+
+
 def dft_table():
-    sample = np.arange(LENGTH)[:, None]
-    bins = np.arange(BINS)[None, :]
-    angle = np.mod(sample * bins, LENGTH).astype(np.float64) * (2.0 * np.pi / LENGTH)
-    table = np.concatenate([np.cos(angle), -np.sin(angle)], axis=1).astype(np.float32)
-    return (table.astype(ml_dtypes.bfloat16).astype(np.float32) * np.float32(SCALE)).astype(
-        ml_dtypes.bfloat16
-    )
+    half = np.arange(LENGTH // 2)[:, None]
+    bins = np.arange(HALF)[None, :]
+    tables = []
+    for parity in range(2):
+        angle = angles(2 * half + parity, bins)
+        real, imag = np.cos(angle), -np.sin(angle)
+        middle = angles(2 * half + parity, BINS // 2)[:, 0]
+        imag[:, 0] = -np.sin(middle) if parity else np.cos(middle)
+        tables.append(np.concatenate([real, imag], axis=1).astype(np.float32))
+    table = np.stack(tables).astype(ml_dtypes.bfloat16).astype(np.float32) * np.float32(SCALE)
+    return table.astype(ml_dtypes.bfloat16)
 
 
 def lag_table():
-    bins = np.arange(BINS)[:, None]
+    bins = np.arange(BINS)
+    bins = np.where(bins > HALF, BINS + HALF - bins, bins)[:, None]
     lag = np.arange(LAGS)[None, :] - LAGS // 2
-    angle = np.mod(bins * lag, LENGTH).astype(np.float64) * (2.0 * np.pi / LENGTH)
+    angle = angles(bins, lag)
     weights = np.where(bins == 0, 1.0, 2.0)
     table = np.concatenate([weights * np.cos(angle), -weights * np.sin(angle)], axis=0)
     high, low = split_high_low(table.astype(np.float32))
@@ -80,21 +92,21 @@
         return pltpu.make_async_copy(source, target, sems.at[index])
 
     windows = raw_ref.shape[0] // CHUNKS
-    depth = LENGTH // CHUNKS
+    parts = 2
     raw_copies = [
         fetch(
             raw_hbm.at[pl.ds(windows * c, windows)], raw_ref.at[pl.ds(windows * c, windows)], c
         )
         for c in range(CHUNKS)
     ]
-    fir_copy = fetch(fir_hbm, fir_ref, CHUNKS)
+    fir_copy = fetch(fir_hbm, fir_ref.at[:, pl.ds(0, REACHED)], CHUNKS)
     dft_copies = [
         fetch(
-            dft_hbm.at[pl.ds(depth * c, depth)],
-            dft_ref.at[pl.ds(depth * c, depth)],
+            dft_hbm.at[c],
+            dft_ref.at[c],
             CHUNKS + 1 + c,
         )
-        for c in range(CHUNKS)
+        for c in range(parts)
     ]
     for copy in raw_copies + [fir_copy] + dft_copies:
         copy.start()
@@ -109,24 +121,54 @@
             for k in range(blocks):
                 wide_ref[k, place] = values[:, LANE * k : LANE * (k + 1)]
             wide_ref[blocks, place, :tail] = values[:, LENGTH:]
+    fir_ref[:, REACHED:] = jnp.zeros((DEC, 2 * LANE - REACHED, 2 * LANE), bf16)
     fir_copy.wait()
-    total = jnp.zeros((SENSORS * ROWS, 2 * LANE), f32)
-    for phase in range(DEC):
-        samples = [
-            wide_ref[k, pl.ds(phase, ROWS, stride=DEC), :].astype(bf16) for k in range(blocks + 1)
-        ]
-        stacked = jnp.concatenate(
-            [jnp.concatenate(samples[k : k + 2], axis=1) for k in range(blocks)], axis=0
+    totals = []
+    for part in range(2):
+        first = blocks // 2 * part
+        count = blocks // 2
+        columns = []
+        for phase in range(DEC):
+            pieces = [
+                wide_ref[k, pl.ds(phase, ROWS, stride=DEC), :].astype(bf16)
+                for k in range(first, first + count + 1)
+            ]
+            columns.append(
+                jnp.concatenate(
+                    [jnp.concatenate(pieces[k : k + 2], axis=1) for k in range(count)], axis=0
+                )
+            )
+        totals.append(
+            jnp.dot(
+                jnp.concatenate(columns, axis=1),
+                fir_ref[...].reshape(DEC * 2 * LANE, 2 * LANE),
+                preferred_element_type=f32,
+            )
         )
-        total = total + jnp.dot(stacked, fir_ref[phase], preferred_element_type=f32)
-    summed = (total[:, :LANE] + total[:, LANE:]).astype(bf16)
-    decimated = jnp.concatenate(
-        [summed[ROWS * k : ROWS * (k + 1)] for k in range(blocks)], axis=1
-    )
-    for copy in dft_copies:
-        copy.wait()
-    spectra = jnp.dot(decimated, dft_ref[...], preferred_element_type=f32)
-    out_ref[...] = spectra.astype(bf16)
+    total = jnp.concatenate(totals, axis=0)
+    summed = total[:, :LANE] + total[:, LANE:]
+    turned = pltpu.roll(summed, LANE // 2, 1)
+    lower = lax.broadcasted_iota(jnp.int32, (ROWS, LANE), 1) < LANE // 2
+    samples = ([], [])
+    for k in range(0, blocks, 2):
+        here = slice(ROWS * k, ROWS * (k + 1))
+        there = slice(ROWS * (k + 1), ROWS * (k + 2))
+        samples[0].append(jnp.where(lower, summed[here], turned[there]))
+        samples[1].append(jnp.where(lower, turned[here], summed[there]))
+    sums = []
+    for parity in range(2):
+        decimated = jnp.concatenate(samples[parity], axis=1).astype(bf16)
+        dft_copies[parity].wait()
+        sums.append(jnp.dot(decimated, dft_ref[parity], preferred_element_type=f32))
+    even, odd = sums
+    real_sum = even[:, :HALF] + odd[:, :HALF]
+    real_difference = even[:, :HALF] - odd[:, :HALF]
+    even_imag, odd_imag = even[:, HALF:], odd[:, HALF:]
+    first = lax.broadcasted_iota(jnp.int32, (ROWS, HALF), 1) == 0
+    out_ref[:, :HALF] = real_sum.astype(bf16)
+    out_ref[:, HALF:BINS] = jnp.where(first, even_imag, real_difference).astype(bf16)
+    out_ref[:, BINS : BINS + HALF] = jnp.where(first, 0.0, even_imag + odd_imag).astype(bf16)
+    out_ref[:, BINS + HALF :] = jnp.where(first, odd_imag, odd_imag - even_imag).astype(bf16)
 
 
 def in_hbm(array):
@@ -143,7 +185,7 @@
         out_specs=pl.BlockSpec(memory_space=VMEM),
         scratch_shapes=[
             pltpu.VMEM(raw.shape, bf16),
-            pltpu.VMEM(fir.shape, bf16),
+            pltpu.VMEM((DEC, 2 * LANE, 2 * LANE), bf16),
             pltpu.VMEM(dft.shape, bf16),
             pltpu.VMEM((LENGTH // LANE + 1, DEC * ROWS, LANE), f32),
             pltpu.SemaphoreType.DMA((2 * CHUNKS + 1,)),

time: 31.4 us -> 31 us (0.987)
  Pallas kernels: 7.87 us -> 7.4 us
    pallas_call x1, Pallas kernels: 3.14 us -> 2.66 us  [spectra_of(): pl.pallas_call(spectra_kernel, out_shape=pltpu.VMEM((ROWS, LENGTH), bf16)...]
where the time goes in v5:
time: 31 us; the launch traced here: 30.9 us
  waiting for transfers between devices  14.9 us (48%)
  starting transfers between devices  8.49 us (27%)
  Pallas kernels  7.4 us (24%)
    ppermute x3, waiting for transfers between devices, onward(): lax.ppermute(block, 'tm', [(i, i ^ step) for i in range(lax.axis_size('tm...  8.76 us
    ppermute x4, waiting for transfers between devices, ring(): return lax.ppermute(block, 'tile', [(i, target(i)) for i in range(tiles)])  6.11 us
    ppermute x4, starting transfers between devices, ring(): return lax.ppermute(block, 'tile', [(i, target(i)) for i in range(tiles)])  4.31 us
    ppermute x3, starting transfers between devices, onward(): lax.ppermute(block, 'tm', [(i, i ^ step) for i in range(lax.axis_size('tm...  4.18 us
    pallas_call x1, Pallas kernels, spectra_of(): pl.pallas_call(spectra_kernel, out_shape=pltpu.VMEM((ROWS, LENGTH), bf16)...  2.66 us
    pallas_call x3, Pallas kernels, cross_of(): pl.pallas_call(cross_kernel, out_shape=(pltpu.VMEM((4, PAIRS, LENGTH), bf...  2.23 us
    pallas_call x1, Pallas kernels, lag_of(): pl.pallas_call(lag_kernel, out_shape=jax.ShapeDtypeStruct((2, 4, SENSORS,...  1.55 us
    pallas_call x1, Pallas kernels, messages_of(): pl.pallas_call(message_kernel, out_shape=(pltpu.VMEM((MESSAGE, LENGTH), b...  0.78 us
  transfers between devices with their start and end apart: 7, of which 3 were waited for; matrix products, arithmetic and copies ran while one was open for 0% of the time, Pallas kernels for 8%

profile of v5, /device:TPU:198, one launch (start us, length us, event | category | flops | bytes accessed | tf_op | source)
XLA Modules:
  0.0 30.9 jit_solution(13275388205431054677)
XLA Ops:
  0.0 2.7 %spectra.1.spectra_ref = bf16[128,1024]{1,0:T(8,128)(2,1)S(1)} custom-call(bf16[16,8,4,1039]{3,2,1,0:T(4,128)(2,1)} %raw_hbm.1, bf16[4,144,256]{2,1,0:T(8,128)(2,1)} %constant.15.clone.fir_hbm, bf16[2,512,512]{2,1,0:T(8,128)(2,1)} %constant.16.clone.dft_hbm), custom_call_target="tpu_custom_call" | custom-call | flops 100000 | bytes 10000 | tf_op jit(solution)/shard_map/spectra/pallas_call | solution.py:181
  2.7 0.1 collective-permute-start.1
  2.8 0.9 %collective-permute-start = (bf16[128,1024]{1,0:T(8,128)(2,1)S(1)}, bf16[128,1024]{1,0:T(8,128)(2,1)S(1)}, u32[]{:S(2)}, u32[]{:S(2)}) collective-permute-start(bf16[128,1024]{1,0:T(8,128)(2,1)S(1)} %spectra.1.spectra_ref), channel_id=1, source_target_pairs={{0,4},{4,12},{8,0},{12,20},{16,8},{20,28},{24,16},{28,36},{32,24},... | collective-permute-start | bytes 786440 | tf_op jit(solution)/shard_map/ppermute | solution.py:422
  3.7 3.3 %collective-permute-start.3 = (bf16[128,1024]{1,0:T(8,128)(2,1)S(1)}, bf16[128,1024]{1,0:T(8,128)(2,1)S(1)}, u32[]{:S(2)}, u32[]{:S(2)}) collective-permute-start(bf16[128,1024]{1,0:T(8,128)(2,1)S(1)} %spectra.1.spectra_ref), channel_id=1, source_target_pairs={{0,8},{4,0},{8,16},{12,4},{16,24},{20,12},{24,32},{28,20},{32,40},... | collective-permute-start | bytes 786440 | tf_op jit(solution)/shard_map/ppermute | solution.py:422
  7.0 0.2 own.1
  7.2 0.0 collective-permute-done.1.far_ref
  7.2 0.7 %cross.3 = (bf16[4,16,1024]{2,1,0:T(8,128)(2,1)S(1)}, f32[8,512]{1,0:T(8,128)S(1)}) custom-call(f32[128,1024]{1,0:T(8,128)S(1)} %get-tuple-element.19.own_ref, bf16[128,1024]{1,0:T(8,128)(2,1)S(1)} %collective-permute-done.1.far_ref), custom_call_target="tpu_custom_call" | custom-call | flops 100000 | bytes 10000 | tf_op jit(solution)/shard_map/cross/pallas_call | solution.py:250
  7.9 6.1 %collective-permute-done.far_ref = bf16[128,1024]{1,0:T(8,128)(2,1)S(1)} collective-permute-done((bf16[128,1024]{1,0:T(8,128)(2,1)S(1)}, bf16[128,1024]{1,0:T(8,128)(2,1)S(1)}, u32[]{:S(2)}, u32[]{:S(2)}) %collective-permute-start) | collective-permute-done | bytes 262176 | tf_op jit(solution)/shard_map/ppermute | solution.py:422
  14.0 0.0 collective-permute-start.2
  14.0 0.7 %cross.4 = (bf16[4,16,1024]{2,1,0:T(8,128)(2,1)S(1)}, f32[8,512]{1,0:T(8,128)S(1)}) custom-call(f32[128,1024]{1,0:T(8,128)S(1)} %get-tuple-element.19.own_ref, bf16[128,1024]{1,0:T(8,128)(2,1)S(1)} %collective-permute-done.far_ref), custom_call_target="tpu_custom_call" | custom-call | flops 100000 | bytes 10000 | tf_op jit(solution)/shard_map/cross/pallas_call | solution.py:250
  14.8 0.0 copy-start
  14.8 0.0 copy-start.1
  14.8 0.0 copy-start.2
  14.8 0.0 collective-permute-done.3.far_ref
  14.8 0.7 %cross.5 = (bf16[4,16,1024]{2,1,0:T(8,128)(2,1)S(1)}, f32[8,512]{1,0:T(8,128)S(1)}) custom-call(f32[128,1024]{1,0:T(8,128)S(1)} %get-tuple-element.19.own_ref, bf16[128,1024]{1,0:T(8,128)(2,1)S(1)} %collective-permute-done.3.far_ref), custom_call_target="tpu_custom_call" | custom-call | flops 100000 | bytes 10000 | tf_op jit(solution)/shard_map/cross/pallas_call | solution.py:250
  15.6 0.0 collective-permute-done.2.far_ref
  15.6 0.8 %message.1 = (bf16[88,1024]{1,0:T(8,128)(2,1)S(1)}, bf16[88,1024]{1,0:T(8,128)(2,1)S(1)}, bf16[88,1024]{1,0:T(8,128)(2,1)S(1)}, bf16[88,1024]{1,0:T(8,128)(2,1)S(1)}) custom-call(f32[128,1024]{1,0:T(8,128)S(1)} %get-tuple-element.19.own_ref, bf16[128,1024]{1,0:T(8,128)(2,1)S(1)} %collective-permute-done.2.far_ref, ...), custom_call_target="tpu_custom_call" | custom-call | flops 100000 | bytes 10000 | tf_op jit(solution)/shard_map/message/pallas_call | solution.py:330
  16.4 3.1 %collective-permute-start.4 = (bf16[88,1024]{1,0:T(8,128)(2,1)S(1)}, bf16[88,1024]{1,0:T(8,128)(2,1)S(1)}, u32[]{:S(2)}, u32[]{:S(2)}) collective-permute-start(bf16[88,1024]{1,0:T(8,128)(2,1)S(1)} %get-tuple-element.30), channel_id=1, source_target_pairs={{0,3},{1,2},{2,1},{3,0},{4,7},{5,6},{6,5},{7,4},{8,11},{9,10},{10,... | collective-permute-start | bytes 540680 | tf_op jit(solution)/shard_map/ppermute | solution.py:425
  19.5 0.6 %collective-permute-start.5 = (bf16[88,1024]{1,0:T(8,128)(2,1)S(1)}, bf16[88,1024]{1,0:T(8,128)(2,1)S(1)}, u32[]{:S(2)}, u32[]{:S(2)}) collective-permute-start(bf16[88,1024]{1,0:T(8,128)(2,1)S(1)} %get-tuple-element.31), channel_id=1, source_target_pairs={{0,2},{1,3},{2,0},{3,1},{4,6},{5,7},{6,4},{7,5},{8,10},{9,11},{10,... | collective-permute-start | bytes 540680 | tf_op jit(solution)/shard_map/ppermute | solution.py:425
  20.1 0.4 %collective-permute-start.6 = (bf16[88,1024]{1,0:T(8,128)(2,1)S(1)}, bf16[88,1024]{1,0:T(8,128)(2,1)S(1)}, u32[]{:S(2)}, u32[]{:S(2)}) collective-permute-start(bf16[88,1024]{1,0:T(8,128)(2,1)S(1)} %get-tuple-element.32), channel_id=1, source_target_pairs={{0,1},{1,0},{2,3},{3,2},{4,5},{5,4},{6,7},{7,6},{8,9},{9,8},{10,11... | collective-permute-start | bytes 540680 | tf_op jit(solution)/shard_map/ppermute | solution.py:425
  20.6 8.0 %collective-permute-done.4.refs_1_ = bf16[88,1024]{1,0:T(8,128)(2,1)S(1)} collective-permute-done((bf16[88,1024]{1,0:T(8,128)(2,1)S(1)}, bf16[88,1024]{1,0:T(8,128)(2,1)S(1)}, u32[]{:S(2)}, u32[]{:S(2)}) %collective-permute-start.4) | collective-permute-done | bytes 180256 | tf_op jit(solution)/shard_map/ppermute | solution.py:425
  28.6 0.0 collective-permute-done.5.refs_2_
  28.6 0.7 %collective-permute-done.6.refs_3_ = bf16[88,1024]{1,0:T(8,128)(2,1)S(1)} collective-permute-done((bf16[88,1024]{1,0:T(8,128)(2,1)S(1)}, bf16[88,1024]{1,0:T(8,128)(2,1)S(1)}, u32[]{:S(2)}, u32[]{:S(2)}) %collective-permute-start.6) | collective-permute-done | bytes 180256 | tf_op jit(solution)/shard_map/ppermute | solution.py:425
  29.3 1.5 %lag.1 = f32[2,4,8,512]{3,2,1,0:T(8,128)} custom-call(s32[1]{0:T(128)} %bitcast.tile_ref, s32[4]{0:T(128)S(1)} %copy-done.2, s32[2,4,8]{2,1,0:T(4,128)S(1)} %copy-done.1, bf16[1,1024,512]{2,1,0:T(8,128)(2,1)S(1)} %copy-done, bf16[88,1024]{1,0:T(8,128)(2,1)S(1)} %get-tuple-element.29.refs_0_, bf16[88,1024]{1,0:T(8,128)(2,1)S(1)} %collective-permute-done.4.refs_1_, ...), custom_call_target="tpu_custom_call" | custom-call | flops 100000 | bytes 10000 | tf_op jit(solution)/shard_map/lag/pallas_call | solution.py:400
  (3 shorter events, 0.0 us)
Async XLA Ops:
  2.7 4.5 %collective-permute-start.1 = (bf16[128,1024]{1,0:T(8,128)(2,1)S(1)}, bf16[128,1024]{1,0:T(8,128)(2,1)S(1)}, u32[]{:S(2)}, u32[]{:S(2)}) collective-permute-start(bf16[128,1024]{1,0:T(8,128)(2,1)S(1)} %spectra.1.spectra_ref), channel_id=1, source_target_pairs={{0,4},{4,0},{8,12},{12,8},{16,20},{20,16},{24,28},{28,24},{32,36},... | collective-permute-start | bytes 786440 | tf_op jit(solution)/shard_map/ppermute | solution.py:422
  2.8 11.3 %collective-permute-start = (bf16[128,1024]{1,0:T(8,128)(2,1)S(1)}, bf16[128,1024]{1,0:T(8,128)(2,1)S(1)}, u32[]{:S(2)}, u32[]{:S(2)}) collective-permute-start(bf16[128,1024]{1,0:T(8,128)(2,1)S(1)} %spectra.1.spectra_ref), channel_id=1, source_target_pairs={{0,4},{4,12},{8,0},{12,20},{16,8},{20,28},{24,16},{28,36},{32,24},... | collective-permute-start | bytes 786440 | tf_op jit(solution)/shard_map/ppermute | solution.py:422
  3.7 11.1 %collective-permute-start.3 = (bf16[128,1024]{1,0:T(8,128)(2,1)S(1)}, bf16[128,1024]{1,0:T(8,128)(2,1)S(1)}, u32[]{:S(2)}, u32[]{:S(2)}) collective-permute-start(bf16[128,1024]{1,0:T(8,128)(2,1)S(1)} %spectra.1.spectra_ref), channel_id=1, source_target_pairs={{0,8},{4,0},{8,16},{12,4},{16,24},{20,12},{24,32},{28,20},{32,40},... | collective-permute-start | bytes 786440 | tf_op jit(solution)/shard_map/ppermute | solution.py:422
  14.0 1.6 %collective-permute-start.2 = (bf16[128,1024]{1,0:T(8,128)(2,1)S(1)}, bf16[128,1024]{1,0:T(8,128)(2,1)S(1)}, u32[]{:S(2)}, u32[]{:S(2)}) collective-permute-start(bf16[128,1024]{1,0:T(8,128)(2,1)S(1)} %collective-permute-done.far_ref), channel_id=1, source_target_pairs={{0,4},{4,0},{8,12},{12,8},{16,20},{20,16},{24,28},{28,24},{32,36},... | collective-permute-start | bytes 786440 | tf_op jit(solution)/shard_map/ppermute | solution.py:422
  14.8 14.5 %copy-start = (bf16[1,1024,512]{2,1,0:T(8,128)(2,1)S(1)}, bf16[1,1024,512]{2,1,0:T(8,128)(2,1)}, u32[]{:S(2)}) copy-start(bf16[1,1024,512]{2,1,0:T(8,128)(2,1)} %constant.17.clone.table_ref) | copy-start | bytes 3145732
  14.8 14.5 %copy-start.1 = (s32[2,4,8]{2,1,0:T(4,128)S(1)}, s32[2,4,8]{2,1,0:T(4,128)}, u32[]{:S(2)}) copy-start(s32[2,4,8]{2,1,0:T(4,128)} %mask_ref.1) | copy-start | bytes 772
  14.8 14.5 %copy-start.2 = (s32[4]{0:T(128)S(1)}, s32[4]{0:T(128)}, u32[]{:S(2)}) copy-start(s32[4]{0:T(128)} %blocks_ref.1) | copy-start | bytes 52
  16.4 12.2 %collective-permute-start.4 = (bf16[88,1024]{1,0:T(8,128)(2,1)S(1)}, bf16[88,1024]{1,0:T(8,128)(2,1)S(1)}, u32[]{:S(2)}, u32[]{:S(2)}) collective-permute-start(bf16[88,1024]{1,0:T(8,128)(2,1)S(1)} %get-tuple-element.30), channel_id=1, source_target_pairs={{0,3},{1,2},{2,1},{3,0},{4,7},{5,6},{6,5},{7,4},{8,11},{9,10},{10,... | collective-permute-start | bytes 540680 | tf_op jit(solution)/shard_map/ppermute | solution.py:425
  19.5 9.1 %collective-permute-start.5 = (bf16[88,1024]{1,0:T(8,128)(2,1)S(1)}, bf16[88,1024]{1,0:T(8,128)(2,1)S(1)}, u32[]{:S(2)}, u32[]{:S(2)}) collective-permute-start(bf16[88,1024]{1,0:T(8,128)(2,1)S(1)} %get-tuple-element.31), channel_id=1, source_target_pairs={{0,2},{1,3},{2,0},{3,1},{4,6},{5,7},{6,4},{7,5},{8,10},{9,11},{10,... | collective-permute-start | bytes 540680 | tf_op jit(solution)/shard_map/ppermute | solution.py:425
  20.1 9.2 %collective-permute-start.6 = (bf16[88,1024]{1,0:T(8,128)(2,1)S(1)}, bf16[88,1024]{1,0:T(8,128)(2,1)S(1)}, u32[]{:S(2)}, u32[]{:S(2)}) collective-permute-start(bf16[88,1024]{1,0:T(8,128)(2,1)S(1)} %get-tuple-element.32), channel_id=1, source_target_pairs={{0,1},{1,0},{2,3},{3,2},{4,5},{5,4},{6,7},{7,6},{8,9},{9,8},{10,11... | collective-permute-start | bytes 540680 | tf_op jit(solution)/shard_map/ppermute | solution.py:425

commit v6 on v5

--- a/solution.py
+++ b/solution.py
@@ -28,7 +28,6 @@
 MESSAGE = CANDS * PAIRS + 16 + SENSORS
 VMEM = pltpu.MemorySpace.VMEM
 CHUNKS = 4
-LAG_PASSES = 2
 LIMIT = 16 * 1024 * 1024
 bf16 = jnp.bfloat16
 f32 = jnp.float32
@@ -81,8 +80,7 @@
     angle = angles(bins, lag)
     weights = np.where(bins == 0, 1.0, 2.0)
     table = np.concatenate([weights * np.cos(angle), -weights * np.sin(angle)], axis=0)
-    high, low = split_high_low(table.astype(np.float32))
-    return np.stack([high, low])
+    return table.astype(np.float32).astype(ml_dtypes.bfloat16)
 
 
 def spectra_kernel(
@@ -200,25 +198,23 @@
     for tile in range(BINS // LANE):
         real = slice(LANE * tile, LANE * (tile + 1))
         imag = slice(BINS + LANE * tile, BINS + LANE * (tile + 1))
+        both = slice(LENGTH + LANE * tile, LENGTH + LANE * (tile + 1))
 
         def step(pair, totals):
             first, second, third, power = totals
             rows = pl.ds(pl.multiple_of(pair * 16, 16), 16)
-            own_real = own_ref[rows, real]
-            own_imag = own_ref[rows, imag]
             far_real = far_ref[rows, real].astype(f32)
             far_imag = far_ref[rows, imag].astype(f32)
-            own_sum = own_real + own_imag
             far_difference = far_real - far_imag
             first, second, third = list(first), list(second), list(third)
             for half in range(2):
                 part = slice(SENSORS * half, SENSORS * (half + 1))
                 power = power + (far_real[part] * far_real[part] + far_imag[part] * far_imag[part])
                 for i in range(SENSORS):
-                    row = SENSORS * half + i
-                    first[i] = first[i] + own_real[row : row + 1] * far_real[part]
-                    second[i] = second[i] + own_imag[row : row + 1] * far_imag[part]
-                    third[i] = third[i] + own_sum[row : row + 1] * far_difference[part]
+                    row = pl.ds(pair * 16 + SENSORS * half + i, 1)
+                    first[i] = first[i] + own_ref[row, real] * far_real[part]
+                    second[i] = second[i] + own_ref[row, imag] * far_imag[part]
+                    third[i] = third[i] + own_ref[row, both] * far_difference[part]
             return tuple(first), tuple(second), tuple(third), power
 
         zero = jnp.zeros((SENSORS, LANE), f32)
@@ -274,7 +270,8 @@
         swapped = jnp.where(upper, pltpu.roll(block, 2, 0), pltpu.roll(block, SENSORS - 2, 0))
         block = jnp.where(odd, swapped, block)
         block = jnp.where(high, pltpu.roll(block, 4, 0), block)
-        own_ref[rows] = block
+        own_ref[rows, :LENGTH] = block
+        own_ref[rows, LENGTH:] = block[:, :BINS] + block[:, BINS:]
         square = block * block
         power = power + (square[:, :BINS] + square[:, BINS:])
     rounded = power.astype(bf16).astype(f32)
@@ -288,7 +285,7 @@
     return pl.pallas_call(
         own_kernel,
         out_shape=(
-            pltpu.VMEM((ROWS, LENGTH), f32),
+            pltpu.VMEM((ROWS, LENGTH + BINS), f32),
             pltpu.VMEM((4, SENSORS, LENGTH), f32),
         ),
         in_specs=[pl.BlockSpec(memory_space=pltpu.MemorySpace.SMEM), vmem],
@@ -364,15 +361,10 @@
             pieces.append(cross[SENSORS * i : SENSORS * (i + 1)] * factor)
     whitened = jnp.concatenate(pieces, axis=0)
     high = whitened.astype(bf16)
-    if LAG_PASSES == 1:
-        lagged = jnp.dot(high, table_ref[0], preferred_element_type=f32)
-    else:
-        low = (whitened - high.astype(f32)).astype(bf16)
-        both = jnp.concatenate([high, low], axis=0)
-        lagged = jnp.dot(both, table_ref[0], preferred_element_type=f32)
-        lagged = lagged[: CANDS * PAIRS] + lagged[CANDS * PAIRS :]
-        if LAG_PASSES == 3:
-            lagged = lagged + jnp.dot(high, table_ref[1], preferred_element_type=f32)
+    low = (whitened - high.astype(f32)).astype(bf16)
+    both = jnp.concatenate([high, low], axis=0)
+    lagged = jnp.dot(both, table_ref[...], preferred_element_type=f32)
+    lagged = lagged[: CANDS * PAIRS] + lagged[CANDS * PAIRS :]
     lagged_ref[...] = lagged.reshape(CANDS, 2, SENSORS, LAGS)
     normaliser = 1.0 / math.sqrt(4 * WIN * BINS)
     tile = tile_ref[0]
@@ -396,7 +388,7 @@
 def lag_of(tile, blocks, mask, *got):
     smem = pl.BlockSpec(memory_space=pltpu.MemorySpace.SMEM)
     vmem = pl.BlockSpec(memory_space=VMEM)
-    table = lag_table()[: max(1, LAG_PASSES - 1)]
+    table = lag_table()
     return pl.pallas_call(
         lag_kernel,
         out_shape=jax.ShapeDtypeStruct((2, 4, SENSORS, LAGS), f32),
@@ -437,7 +429,7 @@
     messages = messages_of(
         own, corner, s_cross, s_power, a_cross, a_power, b_cross, b_power, mine
     )
-    got = [messages[0]] + [onward(messages[k], k) for k in (3, 2, 1)]
+    got = [messages[0]] + [onward(messages[k], k) for k in (2, 1, 3)]
     return lag_of(tile, blocks, mask, *got)
 
 

time: 31 us -> 30.7 us (level)
    ppermute x3, waiting for transfers between devices: 8.76 us -> 8.41 us  [onward(): lax.ppermute(block, 'tm', [(i, i ^ step) for i in range(lax.axis_size('tm...]
  transfers between devices with their start and end apart: 7 -> 7, of which waited for: 3 -> 4; matrix products, arithmetic and copies ran while one was open for 0% -> 0% of each run, Pallas kernels for 8% -> 7%
where the time goes in v6:
time: 30.7 us; the launch traced here: 30.6 us
  waiting for transfers between devices  14.7 us (48%)
  starting transfers between devices  8.65 us (28%)
  Pallas kernels  7.18 us (23%)
    ppermute x3, waiting for transfers between devices, onward(): lax.ppermute(block, 'tm', [(i, i ^ step) for i in range(lax.axis_size('tm...  8.41 us
    ppermute x4, waiting for transfers between devices, ring(): return lax.ppermute(block, 'tile', [(i, target(i)) for i in range(tiles)])  6.25 us
    ppermute x3, starting transfers between devices, onward(): lax.ppermute(block, 'tm', [(i, i ^ step) for i in range(lax.axis_size('tm...  4.35 us
    ppermute x4, starting transfers between devices, ring(): return lax.ppermute(block, 'tile', [(i, target(i)) for i in range(tiles)])  4.31 us
    pallas_call x1, Pallas kernels, spectra_of(): pl.pallas_call(spectra_kernel, out_shape=pltpu.VMEM((ROWS, LENGTH), bf16)...  2.66 us
    pallas_call x3, Pallas kernels, cross_of(): pl.pallas_call(cross_kernel, out_shape=(pltpu.VMEM((4, PAIRS, LENGTH), bf...  2.08 us
    pallas_call x1, Pallas kernels, lag_of(): pl.pallas_call(lag_kernel, out_shape=jax.ShapeDtypeStruct((2, 4, SENSORS,...  1.55 us
    pallas_call x1, Pallas kernels, messages_of(): pl.pallas_call(message_kernel, out_shape=(pltpu.VMEM((MESSAGE, LENGTH), b...  0.71 us
  transfers between devices with their start and end apart: 7, of which 4 were waited for; matrix products, arithmetic and copies ran while one was open for 0% of the time, Pallas kernels for 7%

profile of v6, /device:TPU:198, one launch (start us, length us, event | category | flops | bytes accessed | tf_op | source)
XLA Modules:
  0.0 30.6 jit_solution(17417814867328786145)
XLA Ops:
  0.0 2.7 %spectra.1.spectra_ref = bf16[128,1024]{1,0:T(8,128)(2,1)S(1)} custom-call(bf16[16,8,4,1039]{3,2,1,0:T(4,128)(2,1)} %raw_hbm.1, bf16[4,144,256]{2,1,0:T(8,128)(2,1)} %constant.15.clone.fir_hbm, bf16[2,512,512]{2,1,0:T(8,128)(2,1)} %constant.16.clone.dft_hbm), custom_call_target="tpu_custom_call" | custom-call | flops 100000 | bytes 10000 | tf_op jit(solution)/shard_map/spectra/pallas_call | solution.py:179
  2.7 0.1 collective-permute-start.1
  2.8 0.9 %collective-permute-start = (bf16[128,1024]{1,0:T(8,128)(2,1)S(1)}, bf16[128,1024]{1,0:T(8,128)(2,1)S(1)}, u32[]{:S(2)}, u32[]{:S(2)}) collective-permute-start(bf16[128,1024]{1,0:T(8,128)(2,1)S(1)} %spectra.1.spectra_ref), channel_id=1, source_target_pairs={{0,4},{4,12},{8,0},{12,20},{16,8},{20,28},{24,16},{28,36},{32,24},... | collective-permute-start | bytes 786440 | tf_op jit(solution)/shard_map/ppermute | solution.py:414
  3.7 3.3 %collective-permute-start.3 = (bf16[128,1024]{1,0:T(8,128)(2,1)S(1)}, bf16[128,1024]{1,0:T(8,128)(2,1)S(1)}, u32[]{:S(2)}, u32[]{:S(2)}) collective-permute-start(bf16[128,1024]{1,0:T(8,128)(2,1)S(1)} %spectra.1.spectra_ref), channel_id=1, source_target_pairs={{0,8},{4,0},{8,16},{12,4},{16,24},{20,12},{24,32},{28,20},{32,40},... | collective-permute-start | bytes 786440 | tf_op jit(solution)/shard_map/ppermute | solution.py:414
  7.0 0.2 own.1
  7.2 0.0 collective-permute-done.1.far_ref
  7.2 0.7 %cross.3 = (bf16[4,16,1024]{2,1,0:T(8,128)(2,1)S(1)}, f32[8,512]{1,0:T(8,128)S(1)}) custom-call(f32[128,1536]{1,0:T(8,128)S(1)} %get-tuple-element.19.own_ref, bf16[128,1024]{1,0:T(8,128)(2,1)S(1)} %collective-permute-done.1.far_ref), custom_call_target="tpu_custom_call" | custom-call | flops 100000 | bytes 10000 | tf_op jit(solution)/shard_map/cross/pallas_call | solution.py:246
  7.9 6.2 %collective-permute-done.far_ref = bf16[128,1024]{1,0:T(8,128)(2,1)S(1)} collective-permute-done((bf16[128,1024]{1,0:T(8,128)(2,1)S(1)}, bf16[128,1024]{1,0:T(8,128)(2,1)S(1)}, u32[]{:S(2)}, u32[]{:S(2)}) %collective-permute-start) | collective-permute-done | bytes 262176 | tf_op jit(solution)/shard_map/ppermute | solution.py:414
  14.0 0.0 collective-permute-start.2
  14.0 0.7 %cross.4 = (bf16[4,16,1024]{2,1,0:T(8,128)(2,1)S(1)}, f32[8,512]{1,0:T(8,128)S(1)}) custom-call(f32[128,1536]{1,0:T(8,128)S(1)} %get-tuple-element.19.own_ref, bf16[128,1024]{1,0:T(8,128)(2,1)S(1)} %collective-permute-done.far_ref), custom_call_target="tpu_custom_call" | custom-call | flops 100000 | bytes 10000 | tf_op jit(solution)/shard_map/cross/pallas_call | solution.py:246
  14.7 0.0 copy-start
  14.7 0.0 copy-start.1
  14.8 0.0 copy-start.2
  14.8 0.0 collective-permute-done.3.far_ref
  14.8 0.7 %cross.5 = (bf16[4,16,1024]{2,1,0:T(8,128)(2,1)S(1)}, f32[8,512]{1,0:T(8,128)S(1)}) custom-call(f32[128,1536]{1,0:T(8,128)S(1)} %get-tuple-element.19.own_ref, bf16[128,1024]{1,0:T(8,128)(2,1)S(1)} %collective-permute-done.3.far_ref), custom_call_target="tpu_custom_call" | custom-call | flops 100000 | bytes 10000 | tf_op jit(solution)/shard_map/cross/pallas_call | solution.py:246
  15.5 0.1 collective-permute-done.2.far_ref
  15.6 0.7 %message.1 = (bf16[88,1024]{1,0:T(8,128)(2,1)S(1)}, bf16[88,1024]{1,0:T(8,128)(2,1)S(1)}, bf16[88,1024]{1,0:T(8,128)(2,1)S(1)}, bf16[88,1024]{1,0:T(8,128)(2,1)S(1)}) custom-call(f32[128,1536]{1,0:T(8,128)S(1)} %get-tuple-element.19.own_ref, bf16[128,1024]{1,0:T(8,128)(2,1)S(1)} %collective-permute-done.2.far_ref, ...), custom_call_target="tpu_custom_call" | custom-call | flops 100000 | bytes 10000 | tf_op jit(solution)/shard_map/message/pallas_call | solution.py:327
  16.3 3.3 %collective-permute-start.4 = (bf16[88,1024]{1,0:T(8,128)(2,1)S(1)}, bf16[88,1024]{1,0:T(8,128)(2,1)S(1)}, u32[]{:S(2)}, u32[]{:S(2)}) collective-permute-start(bf16[88,1024]{1,0:T(8,128)(2,1)S(1)} %get-tuple-element.30), channel_id=1, source_target_pairs={{0,2},{1,3},{2,0},{3,1},{4,6},{5,7},{6,4},{7,5},{8,10},{9,11},{10,... | collective-permute-start | bytes 540680 | tf_op jit(solution)/shard_map/ppermute | solution.py:417
  19.6 0.7 %collective-permute-start.5 = (bf16[88,1024]{1,0:T(8,128)(2,1)S(1)}, bf16[88,1024]{1,0:T(8,128)(2,1)S(1)}, u32[]{:S(2)}, u32[]{:S(2)}) collective-permute-start(bf16[88,1024]{1,0:T(8,128)(2,1)S(1)} %get-tuple-element.31), channel_id=1, source_target_pairs={{0,1},{1,0},{2,3},{3,2},{4,5},{5,4},{6,7},{7,6},{8,9},{9,8},{10,11... | collective-permute-start | bytes 540680 | tf_op jit(solution)/shard_map/ppermute | solution.py:417
  20.3 0.4 %collective-permute-start.6 = (bf16[88,1024]{1,0:T(8,128)(2,1)S(1)}, bf16[88,1024]{1,0:T(8,128)(2,1)S(1)}, u32[]{:S(2)}, u32[]{:S(2)}) collective-permute-start(bf16[88,1024]{1,0:T(8,128)(2,1)S(1)} %get-tuple-element.32), channel_id=1, source_target_pairs={{0,3},{1,2},{2,1},{3,0},{4,7},{5,6},{6,5},{7,4},{8,11},{9,10},{10,... | collective-permute-start | bytes 540680 | tf_op jit(solution)/shard_map/ppermute | solution.py:417
  20.6 4.6 %collective-permute-done.4.refs_1_ = bf16[88,1024]{1,0:T(8,128)(2,1)S(1)} collective-permute-done((bf16[88,1024]{1,0:T(8,128)(2,1)S(1)}, bf16[88,1024]{1,0:T(8,128)(2,1)S(1)}, u32[]{:S(2)}, u32[]{:S(2)}) %collective-permute-start.4) | collective-permute-done | bytes 180256 | tf_op jit(solution)/shard_map/ppermute | solution.py:417
  25.2 3.8 %collective-permute-done.5.refs_2_ = bf16[88,1024]{1,0:T(8,128)(2,1)S(1)} collective-permute-done((bf16[88,1024]{1,0:T(8,128)(2,1)S(1)}, bf16[88,1024]{1,0:T(8,128)(2,1)S(1)}, u32[]{:S(2)}, u32[]{:S(2)}) %collective-permute-start.5) | collective-permute-done | bytes 180256 | tf_op jit(solution)/shard_map/ppermute | solution.py:417
  29.0 0.0 collective-permute-done.6.refs_3_
  29.1 1.5 %lag.1 = f32[2,4,8,512]{3,2,1,0:T(8,128)} custom-call(s32[1]{0:T(128)} %bitcast.tile_ref, s32[4]{0:T(128)S(1)} %copy-done.2, s32[2,4,8]{2,1,0:T(4,128)S(1)} %copy-done.1, bf16[1024,512]{1,0:T(8,128)(2,1)S(1)} %copy-done, bf16[88,1024]{1,0:T(8,128)(2,1)S(1)} %get-tuple-element.29.refs_0_, bf16[88,1024]{1,0:T(8,128)(2,1)S(1)} %collective-permute-done.4.refs_1_, ...), custom_call_target="tpu_custom_call" | custom-call | flops 100000 | bytes 10000 | tf_op jit(solution)/shard_map/lag/pallas_call | solution.py:392
  (3 shorter events, 0.0 us)
Async XLA Ops:
  2.7 4.5 %collective-permute-start.1 = (bf16[128,1024]{1,0:T(8,128)(2,1)S(1)}, bf16[128,1024]{1,0:T(8,128)(2,1)S(1)}, u32[]{:S(2)}, u32[]{:S(2)}) collective-permute-start(bf16[128,1024]{1,0:T(8,128)(2,1)S(1)} %spectra.1.spectra_ref), channel_id=1, source_target_pairs={{0,4},{4,0},{8,12},{12,8},{16,20},{20,16},{24,28},{28,24},{32,36},... | collective-permute-start | bytes 786440 | tf_op jit(solution)/shard_map/ppermute | solution.py:414
  2.8 11.3 %collective-permute-start = (bf16[128,1024]{1,0:T(8,128)(2,1)S(1)}, bf16[128,1024]{1,0:T(8,128)(2,1)S(1)}, u32[]{:S(2)}, u32[]{:S(2)}) collective-permute-start(bf16[128,1024]{1,0:T(8,128)(2,1)S(1)} %spectra.1.spectra_ref), channel_id=1, source_target_pairs={{0,4},{4,12},{8,0},{12,20},{16,8},{20,28},{24,16},{28,36},{32,24},... | collective-permute-start | bytes 786440 | tf_op jit(solution)/shard_map/ppermute | solution.py:414
  3.7 11.1 %collective-permute-start.3 = (bf16[128,1024]{1,0:T(8,128)(2,1)S(1)}, bf16[128,1024]{1,0:T(8,128)(2,1)S(1)}, u32[]{:S(2)}, u32[]{:S(2)}) collective-permute-start(bf16[128,1024]{1,0:T(8,128)(2,1)S(1)} %spectra.1.spectra_ref), channel_id=1, source_target_pairs={{0,8},{4,0},{8,16},{12,4},{16,24},{20,12},{24,32},{28,20},{32,40},... | collective-permute-start | bytes 786440 | tf_op jit(solution)/shard_map/ppermute | solution.py:414
  14.0 1.5 %collective-permute-start.2 = (bf16[128,1024]{1,0:T(8,128)(2,1)S(1)}, bf16[128,1024]{1,0:T(8,128)(2,1)S(1)}, u32[]{:S(2)}, u32[]{:S(2)}) collective-permute-start(bf16[128,1024]{1,0:T(8,128)(2,1)S(1)} %collective-permute-done.far_ref), channel_id=1, source_target_pairs={{0,4},{4,0},{8,12},{12,8},{16,20},{20,16},{24,28},{28,24},{32,36},... | collective-permute-start | bytes 786440 | tf_op jit(solution)/shard_map/ppermute | solution.py:414
  14.7 14.3 %copy-start = (bf16[1024,512]{1,0:T(8,128)(2,1)S(1)}, bf16[1024,512]{1,0:T(8,128)(2,1)}, u32[]{:S(2)}) copy-start(bf16[1024,512]{1,0:T(8,128)(2,1)} %constant.17.clone.table_ref) | copy-start | bytes 3145732
  14.7 14.3 %copy-start.1 = (s32[2,4,8]{2,1,0:T(4,128)S(1)}, s32[2,4,8]{2,1,0:T(4,128)}, u32[]{:S(2)}) copy-start(s32[2,4,8]{2,1,0:T(4,128)} %mask_ref.1) | copy-start | bytes 772
  14.8 14.3 %copy-start.2 = (s32[4]{0:T(128)S(1)}, s32[4]{0:T(128)}, u32[]{:S(2)}) copy-start(s32[4]{0:T(128)} %blocks_ref.1) | copy-start | bytes 52
  16.3 8.9 %collective-permute-start.4 = (bf16[88,1024]{1,0:T(8,128)(2,1)S(1)}, bf16[88,1024]{1,0:T(8,128)(2,1)S(1)}, u32[]{:S(2)}, u32[]{:S(2)}) collective-permute-start(bf16[88,1024]{1,0:T(8,128)(2,1)S(1)} %get-tuple-element.30), channel_id=1, source_target_pairs={{0,2},{1,3},{2,0},{3,1},{4,6},{5,7},{6,4},{7,5},{8,10},{9,11},{10,... | collective-permute-start | bytes 540680 | tf_op jit(solution)/shard_map/ppermute | solution.py:417
  19.6 9.5 %collective-permute-start.5 = (bf16[88,1024]{1,0:T(8,128)(2,1)S(1)}, bf16[88,1024]{1,0:T(8,128)(2,1)S(1)}, u32[]{:S(2)}, u32[]{:S(2)}) collective-permute-start(bf16[88,1024]{1,0:T(8,128)(2,1)S(1)} %get-tuple-element.31), channel_id=1, source_target_pairs={{0,1},{1,0},{2,3},{3,2},{4,5},{5,4},{6,7},{7,6},{8,9},{9,8},{10,11... | collective-permute-start | bytes 540680 | tf_op jit(solution)/shard_map/ppermute | solution.py:417
  20.3 8.8 %collective-permute-start.6 = (bf16[88,1024]{1,0:T(8,128)(2,1)S(1)}, bf16[88,1024]{1,0:T(8,128)(2,1)S(1)}, u32[]{:S(2)}, u32[]{:S(2)}) collective-permute-start(bf16[88,1024]{1,0:T(8,128)(2,1)S(1)} %get-tuple-element.32), channel_id=1, source_target_pairs={{0,3},{1,2},{2,1},{3,0},{4,7},{5,6},{6,5},{7,4},{8,11},{9,10},{10,... | collective-permute-start | bytes 540680 | tf_op jit(solution)/shard_map/ppermute | solution.py:417

commit v7 on v6

--- a/solution.py
+++ b/solution.py
@@ -106,7 +106,7 @@
         )
         for c in range(parts)
     ]
-    for copy in raw_copies + [fir_copy] + dft_copies:
+    for copy in [fir_copy] + raw_copies + dft_copies:
         copy.start()
     blocks = LENGTH // LANE
     tail = raw_ref.shape[-1] - LENGTH

time: 30.7 us -> 30.8 us (level)
  no operation moved by 1% of the time
where the time goes in v7:
time: 30.8 us; the launch traced here: 30.7 us
  waiting for transfers between devices  14.6 us (47%)
  starting transfers between devices  8.64 us (28%)
  Pallas kernels  7.26 us (24%)
    ppermute x3, waiting for transfers between devices, onward(): lax.ppermute(block, 'tm', [(i, i ^ step) for i in range(lax.axis_size('tm...  8.4 us
    ppermute x4, waiting for transfers between devices, ring(): return lax.ppermute(block, 'tile', [(i, target(i)) for i in range(tiles)])  6.25 us
    ppermute x3, starting transfers between devices, onward(): lax.ppermute(block, 'tm', [(i, i ^ step) for i in range(lax.axis_size('tm...  4.34 us
    ppermute x4, starting transfers between devices, ring(): return lax.ppermute(block, 'tile', [(i, target(i)) for i in range(tiles)])  4.31 us
    pallas_call x1, Pallas kernels, spectra_of(): pl.pallas_call(spectra_kernel, out_shape=pltpu.VMEM((ROWS, LENGTH), bf16)...  2.75 us
    pallas_call x3, Pallas kernels, cross_of(): pl.pallas_call(cross_kernel, out_shape=(pltpu.VMEM((4, PAIRS, LENGTH), bf...  2.08 us
    pallas_call x1, Pallas kernels, lag_of(): pl.pallas_call(lag_kernel, out_shape=jax.ShapeDtypeStruct((2, 4, SENSORS,...  1.54 us
    pallas_call x1, Pallas kernels, messages_of(): pl.pallas_call(message_kernel, out_shape=(pltpu.VMEM((MESSAGE, LENGTH), b...  0.71 us
  transfers between devices with their start and end apart: 7, of which 4 were waited for; matrix products, arithmetic and copies ran while one was open for 0% of the time, Pallas kernels for 7%

profile of v7, /device:TPU:198, one launch (start us, length us, event | category | flops | bytes accessed | tf_op | source)
XLA Modules:
  0.0 30.7 jit_solution(13079777888987228873)
XLA Ops:
  0.0 2.7 %spectra.1.spectra_ref = bf16[128,1024]{1,0:T(8,128)(2,1)S(1)} custom-call(bf16[16,8,4,1039]{3,2,1,0:T(4,128)(2,1)} %raw_hbm.1, bf16[4,144,256]{2,1,0:T(8,128)(2,1)} %constant.15.clone.fir_hbm, bf16[2,512,512]{2,1,0:T(8,128)(2,1)} %constant.16.clone.dft_hbm), custom_call_target="tpu_custom_call" | custom-call | flops 100000 | bytes 10000 | tf_op jit(solution)/shard_map/spectra/pallas_call | solution.py:179
  2.8 0.1 collective-permute-start.1
  2.9 0.9 %collective-permute-start = (bf16[128,1024]{1,0:T(8,128)(2,1)S(1)}, bf16[128,1024]{1,0:T(8,128)(2,1)S(1)}, u32[]{:S(2)}, u32[]{:S(2)}) collective-permute-start(bf16[128,1024]{1,0:T(8,128)(2,1)S(1)} %spectra.1.spectra_ref), channel_id=1, source_target_pairs={{0,4},{4,12},{8,0},{12,20},{16,8},{20,28},{24,16},{28,36},{32,24},... | collective-permute-start | bytes 786440 | tf_op jit(solution)/shard_map/ppermute | solution.py:414
  3.8 3.3 %collective-permute-start.3 = (bf16[128,1024]{1,0:T(8,128)(2,1)S(1)}, bf16[128,1024]{1,0:T(8,128)(2,1)S(1)}, u32[]{:S(2)}, u32[]{:S(2)}) collective-permute-start(bf16[128,1024]{1,0:T(8,128)(2,1)S(1)} %spectra.1.spectra_ref), channel_id=1, source_target_pairs={{0,8},{4,0},{8,16},{12,4},{16,24},{20,12},{24,32},{28,20},{32,40},... | collective-permute-start | bytes 786440 | tf_op jit(solution)/shard_map/ppermute | solution.py:414
  7.1 0.2 own.1
  7.3 0.0 collective-permute-done.1.far_ref
  7.3 0.7 %cross.3 = (bf16[4,16,1024]{2,1,0:T(8,128)(2,1)S(1)}, f32[8,512]{1,0:T(8,128)S(1)}) custom-call(f32[128,1536]{1,0:T(8,128)S(1)} %get-tuple-element.19.own_ref, bf16[128,1024]{1,0:T(8,128)(2,1)S(1)} %collective-permute-done.1.far_ref), custom_call_target="tpu_custom_call" | custom-call | flops 100000 | bytes 10000 | tf_op jit(solution)/shard_map/cross/pallas_call | solution.py:246
  8.0 6.2 %collective-permute-done.far_ref = bf16[128,1024]{1,0:T(8,128)(2,1)S(1)} collective-permute-done((bf16[128,1024]{1,0:T(8,128)(2,1)S(1)}, bf16[128,1024]{1,0:T(8,128)(2,1)S(1)}, u32[]{:S(2)}, u32[]{:S(2)}) %collective-permute-start) | collective-permute-done | bytes 262176 | tf_op jit(solution)/shard_map/ppermute | solution.py:414
  14.1 0.0 collective-permute-start.2
  14.1 0.7 %cross.4 = (bf16[4,16,1024]{2,1,0:T(8,128)(2,1)S(1)}, f32[8,512]{1,0:T(8,128)S(1)}) custom-call(f32[128,1536]{1,0:T(8,128)S(1)} %get-tuple-element.19.own_ref, bf16[128,1024]{1,0:T(8,128)(2,1)S(1)} %collective-permute-done.far_ref), custom_call_target="tpu_custom_call" | custom-call | flops 100000 | bytes 10000 | tf_op jit(solution)/shard_map/cross/pallas_call | solution.py:246
  14.8 0.0 copy-start
  14.8 0.0 copy-start.1
  14.8 0.0 copy-start.2
  14.9 0.0 collective-permute-done.3.far_ref
  14.9 0.7 %cross.5 = (bf16[4,16,1024]{2,1,0:T(8,128)(2,1)S(1)}, f32[8,512]{1,0:T(8,128)S(1)}) custom-call(f32[128,1536]{1,0:T(8,128)S(1)} %get-tuple-element.19.own_ref, bf16[128,1024]{1,0:T(8,128)(2,1)S(1)} %collective-permute-done.3.far_ref), custom_call_target="tpu_custom_call" | custom-call | flops 100000 | bytes 10000 | tf_op jit(solution)/shard_map/cross/pallas_call | solution.py:246
  15.6 0.1 collective-permute-done.2.far_ref
  15.7 0.7 %message.1 = (bf16[88,1024]{1,0:T(8,128)(2,1)S(1)}, bf16[88,1024]{1,0:T(8,128)(2,1)S(1)}, bf16[88,1024]{1,0:T(8,128)(2,1)S(1)}, bf16[88,1024]{1,0:T(8,128)(2,1)S(1)}) custom-call(f32[128,1536]{1,0:T(8,128)S(1)} %get-tuple-element.19.own_ref, bf16[128,1024]{1,0:T(8,128)(2,1)S(1)} %collective-permute-done.2.far_ref, ...), custom_call_target="tpu_custom_call" | custom-call | flops 100000 | bytes 10000 | tf_op jit(solution)/shard_map/message/pallas_call | solution.py:327
  16.4 3.3 %collective-permute-start.4 = (bf16[88,1024]{1,0:T(8,128)(2,1)S(1)}, bf16[88,1024]{1,0:T(8,128)(2,1)S(1)}, u32[]{:S(2)}, u32[]{:S(2)}) collective-permute-start(bf16[88,1024]{1,0:T(8,128)(2,1)S(1)} %get-tuple-element.30), channel_id=1, source_target_pairs={{0,2},{1,3},{2,0},{3,1},{4,6},{5,7},{6,4},{7,5},{8,10},{9,11},{10,... | collective-permute-start | bytes 540680 | tf_op jit(solution)/shard_map/ppermute | solution.py:417
  19.6 0.7 %collective-permute-start.5 = (bf16[88,1024]{1,0:T(8,128)(2,1)S(1)}, bf16[88,1024]{1,0:T(8,128)(2,1)S(1)}, u32[]{:S(2)}, u32[]{:S(2)}) collective-permute-start(bf16[88,1024]{1,0:T(8,128)(2,1)S(1)} %get-tuple-element.31), channel_id=1, source_target_pairs={{0,1},{1,0},{2,3},{3,2},{4,5},{5,4},{6,7},{7,6},{8,9},{9,8},{10,11... | collective-permute-start | bytes 540680 | tf_op jit(solution)/shard_map/ppermute | solution.py:417
  20.3 0.4 %collective-permute-start.6 = (bf16[88,1024]{1,0:T(8,128)(2,1)S(1)}, bf16[88,1024]{1,0:T(8,128)(2,1)S(1)}, u32[]{:S(2)}, u32[]{:S(2)}) collective-permute-start(bf16[88,1024]{1,0:T(8,128)(2,1)S(1)} %get-tuple-element.32), channel_id=1, source_target_pairs={{0,3},{1,2},{2,1},{3,0},{4,7},{5,6},{6,5},{7,4},{8,11},{9,10},{10,... | collective-permute-start | bytes 540680 | tf_op jit(solution)/shard_map/ppermute | solution.py:417
  20.7 4.6 %collective-permute-done.4.refs_1_ = bf16[88,1024]{1,0:T(8,128)(2,1)S(1)} collective-permute-done((bf16[88,1024]{1,0:T(8,128)(2,1)S(1)}, bf16[88,1024]{1,0:T(8,128)(2,1)S(1)}, u32[]{:S(2)}, u32[]{:S(2)}) %collective-permute-start.4) | collective-permute-done | bytes 180256 | tf_op jit(solution)/shard_map/ppermute | solution.py:417
  25.3 3.8 %collective-permute-done.5.refs_2_ = bf16[88,1024]{1,0:T(8,128)(2,1)S(1)} collective-permute-done((bf16[88,1024]{1,0:T(8,128)(2,1)S(1)}, bf16[88,1024]{1,0:T(8,128)(2,1)S(1)}, u32[]{:S(2)}, u32[]{:S(2)}) %collective-permute-start.5) | collective-permute-done | bytes 180256 | tf_op jit(solution)/shard_map/ppermute | solution.py:417
  29.1 0.0 collective-permute-done.6.refs_3_
  29.1 1.5 %lag.1 = f32[2,4,8,512]{3,2,1,0:T(8,128)} custom-call(s32[1]{0:T(128)} %bitcast.tile_ref, s32[4]{0:T(128)S(1)} %copy-done.2, s32[2,4,8]{2,1,0:T(4,128)S(1)} %copy-done.1, bf16[1024,512]{1,0:T(8,128)(2,1)S(1)} %copy-done, bf16[88,1024]{1,0:T(8,128)(2,1)S(1)} %get-tuple-element.29.refs_0_, bf16[88,1024]{1,0:T(8,128)(2,1)S(1)} %collective-permute-done.4.refs_1_, ...), custom_call_target="tpu_custom_call" | custom-call | flops 100000 | bytes 10000 | tf_op jit(solution)/shard_map/lag/pallas_call | solution.py:392
  (3 shorter events, 0.0 us)
Async XLA Ops:
  2.8 4.5 %collective-permute-start.1 = (bf16[128,1024]{1,0:T(8,128)(2,1)S(1)}, bf16[128,1024]{1,0:T(8,128)(2,1)S(1)}, u32[]{:S(2)}, u32[]{:S(2)}) collective-permute-start(bf16[128,1024]{1,0:T(8,128)(2,1)S(1)} %spectra.1.spectra_ref), channel_id=1, source_target_pairs={{0,4},{4,0},{8,12},{12,8},{16,20},{20,16},{24,28},{28,24},{32,36},... | collective-permute-start | bytes 786440 | tf_op jit(solution)/shard_map/ppermute | solution.py:414
  2.9 11.3 %collective-permute-start = (bf16[128,1024]{1,0:T(8,128)(2,1)S(1)}, bf16[128,1024]{1,0:T(8,128)(2,1)S(1)}, u32[]{:S(2)}, u32[]{:S(2)}) collective-permute-start(bf16[128,1024]{1,0:T(8,128)(2,1)S(1)} %spectra.1.spectra_ref), channel_id=1, source_target_pairs={{0,4},{4,12},{8,0},{12,20},{16,8},{20,28},{24,16},{28,36},{32,24},... | collective-permute-start | bytes 786440 | tf_op jit(solution)/shard_map/ppermute | solution.py:414
  3.8 11.1 %collective-permute-start.3 = (bf16[128,1024]{1,0:T(8,128)(2,1)S(1)}, bf16[128,1024]{1,0:T(8,128)(2,1)S(1)}, u32[]{:S(2)}, u32[]{:S(2)}) collective-permute-start(bf16[128,1024]{1,0:T(8,128)(2,1)S(1)} %spectra.1.spectra_ref), channel_id=1, source_target_pairs={{0,8},{4,0},{8,16},{12,4},{16,24},{20,12},{24,32},{28,20},{32,40},... | collective-permute-start | bytes 786440 | tf_op jit(solution)/shard_map/ppermute | solution.py:414
  14.1 1.5 %collective-permute-start.2 = (bf16[128,1024]{1,0:T(8,128)(2,1)S(1)}, bf16[128,1024]{1,0:T(8,128)(2,1)S(1)}, u32[]{:S(2)}, u32[]{:S(2)}) collective-permute-start(bf16[128,1024]{1,0:T(8,128)(2,1)S(1)} %collective-permute-done.far_ref), channel_id=1, source_target_pairs={{0,4},{4,0},{8,12},{12,8},{16,20},{20,16},{24,28},{28,24},{32,36},... | collective-permute-start | bytes 786440 | tf_op jit(solution)/shard_map/ppermute | solution.py:414
  14.8 14.3 %copy-start = (bf16[1024,512]{1,0:T(8,128)(2,1)S(1)}, bf16[1024,512]{1,0:T(8,128)(2,1)}, u32[]{:S(2)}) copy-start(bf16[1024,512]{1,0:T(8,128)(2,1)} %constant.17.clone.table_ref) | copy-start | bytes 3145732
  14.8 14.3 %copy-start.1 = (s32[2,4,8]{2,1,0:T(4,128)S(1)}, s32[2,4,8]{2,1,0:T(4,128)}, u32[]{:S(2)}) copy-start(s32[2,4,8]{2,1,0:T(4,128)} %mask_ref.1) | copy-start | bytes 772
  14.8 14.3 %copy-start.2 = (s32[4]{0:T(128)S(1)}, s32[4]{0:T(128)}, u32[]{:S(2)}) copy-start(s32[4]{0:T(128)} %blocks_ref.1) | copy-start | bytes 52
  16.4 8.9 %collective-permute-start.4 = (bf16[88,1024]{1,0:T(8,128)(2,1)S(1)}, bf16[88,1024]{1,0:T(8,128)(2,1)S(1)}, u32[]{:S(2)}, u32[]{:S(2)}) collective-permute-start(bf16[88,1024]{1,0:T(8,128)(2,1)S(1)} %get-tuple-element.30), channel_id=1, source_target_pairs={{0,2},{1,3},{2,0},{3,1},{4,6},{5,7},{6,4},{7,5},{8,10},{9,11},{10,... | collective-permute-start | bytes 540680 | tf_op jit(solution)/shard_map/ppermute | solution.py:417
  19.6 9.5 %collective-permute-start.5 = (bf16[88,1024]{1,0:T(8,128)(2,1)S(1)}, bf16[88,1024]{1,0:T(8,128)(2,1)S(1)}, u32[]{:S(2)}, u32[]{:S(2)}) collective-permute-start(bf16[88,1024]{1,0:T(8,128)(2,1)S(1)} %get-tuple-element.31), channel_id=1, source_target_pairs={{0,1},{1,0},{2,3},{3,2},{4,5},{5,4},{6,7},{7,6},{8,9},{9,8},{10,11... | collective-permute-start | bytes 540680 | tf_op jit(solution)/shard_map/ppermute | solution.py:417
  20.3 8.8 %collective-permute-start.6 = (bf16[88,1024]{1,0:T(8,128)(2,1)S(1)}, bf16[88,1024]{1,0:T(8,128)(2,1)S(1)}, u32[]{:S(2)}, u32[]{:S(2)}) collective-permute-start(bf16[88,1024]{1,0:T(8,128)(2,1)S(1)} %get-tuple-element.32), channel_id=1, source_target_pairs={{0,3},{1,2},{2,1},{3,0},{4,7},{5,6},{6,5},{7,4},{8,11},{9,10},{10,... | collective-permute-start | bytes 540680 | tf_op jit(solution)/shard_map/ppermute | solution.py:417
